TPU v7x, 32 devices: a whole 2x2x4 slice. The times are simulated.
32 devices in a mesh: dp: 16 (over z, y, core), mp: 2 (over x).
Axes of the slice: x: 2, y: 2, z: 4, core: 2. Of those that a mesh axis runs over, the one named last changes fastest.
Arguments:
- tokens: bfloat16 [2, 9856, 1024], P(None, ('dp', 'mp')), may hold values from -6 to 6
- segments: int32 [2, 9856], P(None, 'dp'), may hold values from 0 to 7, as said below
- qkv_weight: bfloat16 [2, 3, 1024, 1024], P(None, None, 'dp', 'mp'), may hold values from -0.1875 to 0.1875
- out_weight: bfloat16 [2, 1024, 1024], P(None, 'mp', 'dp'), may hold values from -0.75 to 0.75
- up_weight: bfloat16 [2, 1024, 4096], P(None, 'dp', 'mp'), may hold values from -0.1875 to 0.1875
- down_weight: bfloat16 [2, 4096, 1024], P(None, 'mp', 'dp'), may hold values from -0.125 to 0.125
- vectors: bfloat16 [2, 8, 1024], P(None, None, 'dp'), may hold values from -1.2 to 1.6, as said below
- qv_bias: bfloat16 [2, 2, 16, 64], P(None, None, 'mp', 'dp'), may hold values from -3 to 3
- up_bias: bfloat16 [2, 64, 64], P(None, 'mp', 'dp'), may hold values from -3 to 3
- cotangent: bfloat16 [2, 9856, 1024], P(None, ('dp', 'mp')), may hold values from -6 to 6
Outputs:
- output: bfloat16 [2, 9856, 1024], P(None, ('dp', 'mp'))
- tokens_grad: float32 [2, 9856, 1024], P(None, ('dp', 'mp'))
- qkv_grad: float32 [2, 3, 1024, 1024], P(None, None, 'dp', 'mp')
- out_grad: float32 [2, 1024, 1024], P(None, 'mp', 'dp')
- up_grad: float32 [2, 1024, 4096], P(None, 'dp', 'mp')
- down_grad: float32 [2, 4096, 1024], P(None, 'mp', 'dp')
- vectors_grad: float32 [2, 8, 1024], P(None, None, 'dp')
- qv_bias_grad: float32 [2, 2, 16, 64], P(None, None, 'mp', 'dp')
- up_bias_grad: float32 [2, 64, 64], P(None, 'mp', 'dp')
Inputs may be any that keep to these rules, and one draw needn't show every extreme that they name: `segments`: each block of 616 consecutive rows of a micro-batch holds 2 crops of 197 tokens and 6 crops of 37 tokens in a drawn order, numbered 0 upward in order of position. `vectors`: rows 0 and 4 lie in 0.4 to 1.6, rows 3 and 7 in 0.4 to 1.2.
All inputs are finite; a program needn't handle non-finite values.
Results may differ from a plain program's by a relative error of at most 0.019.
Values may be sent and summed in bfloat16 or wider, within the bound.
A program may use at most 320 MiB of HBM per device.

v0:
```python
import math

import jax
import jax.numpy as jnp
from jax import lax
from jax.sharding import PartitionSpec as P

INV_ROOT_TWO = 0.7071067811865476
INV_ROOT_TAU = 0.3989422804014327


def layer_norm(values, gain, shift):
    centred = values - jnp.mean(values, axis=-1, keepdims=True)
    inverse = lax.rsqrt(jnp.mean(centred * centred, axis=-1, keepdims=True) + 1e-06)
    normed = centred * inverse
    return (normed * gain + shift, normed, inverse)


def norm_backward(upstream, normed, inverse, gain):
    scaled = upstream * gain
    inner = (
        scaled
        - jnp.mean(scaled, axis=-1, keepdims=True)
        - normed * jnp.mean(scaled * normed, axis=-1, keepdims=True)
    )
    return (inverse * inner, jnp.sum(upstream * normed, axis=0), jnp.sum(upstream, axis=0))


def contract_rows(left, right):
    return lax.dot_general(
        left, right, (((0,), (0,)), ((), ())), preferred_element_type=jnp.float32
    )


def against_rows(left, right):
    return lax.dot_general(
        left, right, (((1,), (1,)), ((), ())), preferred_element_type=jnp.float32
    )


def gather_normed(values):
    return lax.all_gather(values, "mp", axis=0, tiled=True)


def gather_upstream(values):
    return lax.all_gather(values, "mp", axis=0, tiled=True)


def branch_sum(term, count):
    return lax.psum_scatter(
        term(jnp.int32(0), count * lax.axis_size("mp")).astype(jnp.bfloat16),
        "mp",
        scatter_dimension=0,
        tiled=True,
    ).astype(jnp.float32)


def input_sum(term, count):
    return lax.psum_scatter(
        term(jnp.int32(0), count * lax.axis_size("mp")).astype(jnp.bfloat16),
        "mp",
        scatter_dimension=0,
        tiled=True,
    ).astype(jnp.float32)


def on_device(
    tokens,
    segments,
    qkv_weight,
    out_weight,
    up_weight,
    down_weight,
    vectors,
    qv_bias,
    up_bias,
    cotangent,
):
    layers = qkv_weight.shape[0]
    micro = tokens.shape[0]
    width = tokens.shape[2]
    head_dim = qv_bias.shape[3] * lax.axis_size("dp")
    scale = 1.0 / math.sqrt(head_dim)

    def attention_scores(query, keys, same_crop, heads):
        total_rows = query.shape[0]
        raw = (
            jnp.einsum(
                "qhd,khd->hqk",
                query.reshape(total_rows, heads, -1),
                keys.reshape(total_rows, heads, -1),
                preferred_element_type=jnp.float32,
            )
            * scale
        )
        return jnp.where(same_crop, raw, -1000000000.0)

    def forward_layer(resid, same_crop, whole):
        qkv_full, out_full, up_full, down_full, vector_half, qv_full, up_shift = whole
        vector_rows = vector_half.astype(jnp.float32)
        normed_in, first_normed, first_inverse = layer_norm(resid, vector_rows[0], vector_rows[1])
        first_all = gather_normed(normed_in.astype(jnp.bfloat16))
        total_rows = first_all.shape[0]
        heads = qv_full.shape[1]
        qv_flat = qv_full.astype(jnp.float32).reshape(2, -1)
        query = (
            jnp.dot(first_all, qkv_full[0], preferred_element_type=jnp.float32) + qv_flat[0]
        ).astype(jnp.bfloat16)
        keys = jnp.dot(first_all, qkv_full[1], preferred_element_type=jnp.float32).astype(
            jnp.bfloat16
        )
        values = (
            jnp.dot(first_all, qkv_full[2], preferred_element_type=jnp.float32) + qv_flat[1]
        ).astype(jnp.bfloat16)
        scores = attention_scores(query, keys, same_crop, heads)
        peak = jnp.max(scores, axis=-1, keepdims=True)
        powers = jnp.exp(scores - peak)
        totals = jnp.sum(powers, axis=-1, keepdims=True)
        probs = (powers / totals).astype(jnp.bfloat16)
        log_totals = peak + jnp.log(totals)
        attended = (
            jnp.einsum(
                "hqk,khd->qhd",
                probs,
                values.reshape(total_rows, heads, -1),
                preferred_element_type=jnp.float32,
            )
            .reshape(total_rows, -1)
            .astype(jnp.bfloat16)
        )

        def project_rows(start, size):
            return jnp.dot(attended, out_full, preferred_element_type=jnp.float32)

        projected = branch_sum(project_rows, resid.shape[0])
        middle = resid + vector_rows[3] * (projected + vector_rows[2])
        normed_mid, second_normed, second_inverse = layer_norm(
            middle, vector_rows[4], vector_rows[5]
        )
        second_all = gather_normed(normed_mid.astype(jnp.bfloat16))
        hidden_pre = jnp.dot(
            second_all, up_full, preferred_element_type=jnp.float32
        ) + up_shift.astype(jnp.float32).reshape(-1)
        hidden = (0.5 * hidden_pre * (1.0 + lax.erf(hidden_pre * INV_ROOT_TWO))).astype(
            jnp.bfloat16
        )

        def down_rows(start, size):
            return jnp.dot(hidden, down_full, preferred_element_type=jnp.float32)

        returned = branch_sum(down_rows, resid.shape[0])
        result = middle + vector_rows[7] * (returned + vector_rows[6])
        saved = (
            first_normed,
            first_inverse,
            first_all,
            query,
            keys,
            values,
            log_totals,
            attended,
            projected,
            second_normed,
            second_inverse,
            second_all,
            hidden_pre,
            hidden,
            returned,
        )
        return (result, saved)

    def backward_layer(upstream, same_crop, whole, saved):
        qkv_full, out_full, up_full, down_full, vector_half, qv_full, up_shift = whole
        (
            first_normed,
            first_inverse,
            first_all,
            query,
            keys,
            values,
            log_totals,
            attended,
            projected,
            second_normed,
            second_inverse,
            second_all,
            hidden_pre,
            hidden,
            returned,
        ) = saved
        vector_rows = vector_half.astype(jnp.float32)
        count = upstream.shape[0]
        total_rows = first_all.shape[0]
        heads = qv_full.shape[1]
        scaled_up = vector_rows[7] * upstream
        grad_shift_mlp = jnp.sum(scaled_up, axis=0)
        grad_scale_mlp = jnp.sum(upstream * (returned + vector_rows[6]), axis=0)
        returned_all = gather_upstream(scaled_up.astype(jnp.bfloat16))
        grad_down = contract_rows(hidden, returned_all)
        grad_hidden = against_rows(returned_all, down_full)
        normal_cdf = 0.5 * (1.0 + lax.erf(hidden_pre * INV_ROOT_TWO))
        normal_pdf = jnp.exp(-0.5 * hidden_pre * hidden_pre) * INV_ROOT_TAU
        grad_pre = (grad_hidden * (normal_cdf + hidden_pre * normal_pdf)).astype(jnp.bfloat16)
        grad_up_shift = jnp.sum(grad_pre.astype(jnp.float32), axis=0).reshape(-1, head_dim)
        grad_up = contract_rows(second_all, grad_pre)

        def up_rows(start, size):
            return against_rows(lax.dynamic_slice_in_dim(grad_pre, start, size, 0), up_full)

        grad_second = input_sum(up_rows, count)
        grad_mid_norm, grad_gain_two, grad_shift_two = norm_backward(
            grad_second, second_normed, second_inverse, vector_rows[4]
        )
        grad_middle = upstream + grad_mid_norm
        scaled_mid = vector_rows[3] * grad_middle
        grad_shift_attn = jnp.sum(scaled_mid, axis=0)
        grad_scale_attn = jnp.sum(grad_middle * (projected + vector_rows[2]), axis=0)
        projected_all = gather_upstream(scaled_mid.astype(jnp.bfloat16))
        grad_out = contract_rows(attended, projected_all)
        grad_attended = (
            against_rows(projected_all, out_full)
            .astype(jnp.bfloat16)
            .reshape(total_rows, heads, -1)
        )
        query_heads = query.reshape(total_rows, heads, -1)
        key_heads = keys.reshape(total_rows, heads, -1)
        value_heads = values.reshape(total_rows, heads, -1)
        scores = attention_scores(query, keys, same_crop, heads)
        probs = jnp.exp(scores - log_totals)
        grad_values = jnp.einsum(
            "hqk,qhd->khd",
            probs.astype(jnp.bfloat16),
            grad_attended,
            preferred_element_type=jnp.float32,
        )
        grad_probs = jnp.einsum(
            "qhd,khd->hqk", grad_attended, value_heads, preferred_element_type=jnp.float32
        )
        grad_scores = (
            probs * (grad_probs - jnp.sum(probs * grad_probs, axis=-1, keepdims=True))
        ).astype(jnp.bfloat16)
        grad_query = (
            jnp.einsum("hqk,khd->qhd", grad_scores, key_heads, preferred_element_type=jnp.float32)
            * scale
        )
        grad_keys = (
            jnp.einsum("hqk,qhd->khd", grad_scores, query_heads, preferred_element_type=jnp.float32)
            * scale
        )
        grad_project = (
            jnp.stack([grad_query, grad_keys, grad_values])
            .reshape(3, total_rows, -1)
            .astype(jnp.bfloat16)
        )
        grad_qv = jnp.stack(
            [
                jnp.sum(grad_project[0].astype(jnp.float32), axis=0),
                jnp.sum(grad_project[2].astype(jnp.float32), axis=0),
            ]
        ).reshape(2, heads, head_dim)
        grad_qkv = jnp.einsum(
            "rd,trc->tdc", first_all, grad_project, preferred_element_type=jnp.float32
        )

        def qkv_rows(start, size):
            return jnp.einsum(
                "trc,tdc->rd",
                lax.dynamic_slice_in_dim(grad_project, start, size, 1),
                qkv_full,
                preferred_element_type=jnp.float32,
            )

        grad_first = input_sum(qkv_rows, count)
        grad_in_norm, grad_gain_one, grad_shift_one = norm_backward(
            grad_first, first_normed, first_inverse, vector_rows[0]
        )
        grad_vectors = jnp.stack(
            [
                grad_gain_one,
                grad_shift_one,
                grad_shift_attn,
                grad_scale_attn,
                grad_gain_two,
                grad_shift_two,
                grad_shift_mlp,
                grad_scale_mlp,
            ]
        )
        parts = (grad_qkv, grad_out, grad_up, grad_down, grad_vectors, grad_qv, grad_up_shift)
        return (grad_middle + grad_in_norm, parts)

    shapes = [
        (3, width, qkv_weight.shape[3]),
        (out_weight.shape[1], width),
        (width, up_weight.shape[2]),
        (down_weight.shape[1], width),
        (8, width),
        (2, qv_bias.shape[2], head_dim),
        (up_bias.shape[1], head_dim),
    ]
    zeroed = tuple((jnp.zeros(shape, jnp.float32) for shape in shapes))
    start_sums = tuple((zeroed for layer in range(layers)))

    def one_micro(index, carry):
        sums, out_buffer, grad_buffer = carry
        resid = lax.dynamic_index_in_dim(tokens, index, 0, keepdims=False).astype(jnp.float32)
        crop_ids = lax.dynamic_index_in_dim(segments, index, 0, keepdims=False)
        same_crop = (crop_ids[:, None] == crop_ids[None, :])[None]
        wholes = []
        saves = []
        for layer in range(layers):
            whole = (
                lax.all_gather(qkv_weight[layer], "dp", axis=1, tiled=True),
                lax.all_gather(out_weight[layer], "dp", axis=1, tiled=True),
                lax.all_gather(up_weight[layer], "dp", axis=0, tiled=True),
                lax.all_gather(down_weight[layer], "dp", axis=1, tiled=True),
                lax.all_gather(vectors[layer], "dp", axis=1, tiled=True),
                lax.all_gather(qv_bias[layer], "dp", axis=2, tiled=True),
                lax.all_gather(up_bias[layer], "dp", axis=1, tiled=True),
            )
            resid, saved = forward_layer(resid, same_crop, whole)
            wholes.append(whole)
            saves.append(saved)
        out_buffer = lax.dynamic_update_index_in_dim(
            out_buffer, resid.astype(jnp.bfloat16), index, 0
        )
        upstream = lax.dynamic_index_in_dim(cotangent, index, 0, keepdims=False).astype(jnp.float32)
        new_sums = list(sums)
        for layer in reversed(range(layers)):
            whole = (
                lax.all_gather(qkv_weight[layer], "dp", axis=1, tiled=True),
                lax.all_gather(out_weight[layer], "dp", axis=1, tiled=True),
                lax.all_gather(up_weight[layer], "dp", axis=0, tiled=True),
                lax.all_gather(down_weight[layer], "dp", axis=1, tiled=True),
                lax.all_gather(vectors[layer], "dp", axis=1, tiled=True),
                lax.all_gather(qv_bias[layer], "dp", axis=2, tiled=True),
                lax.all_gather(up_bias[layer], "dp", axis=1, tiled=True),
            )
            upstream, parts = backward_layer(upstream, same_crop, whole, saves[layer])
            new_sums[layer] = tuple((total + piece for total, piece in zip(sums[layer], parts)))
        grad_buffer = lax.dynamic_update_index_in_dim(grad_buffer, upstream, index, 0)
        return (tuple(new_sums), out_buffer, grad_buffer)

    start = (
        start_sums,
        jnp.zeros(tokens.shape, jnp.bfloat16),
        jnp.zeros(tokens.shape, jnp.float32),
    )
    sums, output, tokens_grad = lax.fori_loop(0, micro, one_micro, start)
    reduced = []
    for layer in range(layers):
        totals = sums[layer]
        totals = (
            lax.psum_scatter(
                totals[0].astype(jnp.bfloat16), "dp", scatter_dimension=1, tiled=True
            ).astype(jnp.float32),
            lax.psum_scatter(
                totals[1].astype(jnp.bfloat16), "dp", scatter_dimension=1, tiled=True
            ).astype(jnp.float32),
            lax.psum_scatter(
                totals[2].astype(jnp.bfloat16), "dp", scatter_dimension=0, tiled=True
            ).astype(jnp.float32),
            lax.psum_scatter(
                totals[3].astype(jnp.bfloat16), "dp", scatter_dimension=1, tiled=True
            ).astype(jnp.float32),
            lax.psum_scatter(
                totals[4].astype(jnp.bfloat16), "dp", scatter_dimension=1, tiled=True
            ).astype(jnp.float32),
            lax.psum_scatter(
                totals[5].astype(jnp.bfloat16), "dp", scatter_dimension=2, tiled=True
            ).astype(jnp.float32),
            lax.psum_scatter(
                totals[6].astype(jnp.bfloat16), "dp", scatter_dimension=1, tiled=True
            ).astype(jnp.float32),
        )
        reduced.append(totals)
    stacked = [
        jnp.stack([reduced[layer][member] for layer in range(layers)]) for member in range(7)
    ]
    vector_total = lax.psum(stacked[4], "mp")
    return (
        output,
        tokens_grad,
        stacked[0],
        stacked[1],
        stacked[2],
        stacked[3],
        vector_total,
        stacked[5],
        stacked[6],
    )


def solution(mesh):
    placed = (
        P(None, ("dp", "mp"), None),
        P(None, "dp"),
        P(None, None, "dp", "mp"),
        P(None, "mp", "dp"),
        P(None, "dp", "mp"),
        P(None, "mp", "dp"),
        P(None, None, "dp"),
        P(None, None, "mp", "dp"),
        P(None, "mp", "dp"),
        P(None, ("dp", "mp"), None),
    )
    return jax.shard_map(
        on_device,
        mesh=mesh,
        in_specs=placed,
        out_specs=(
            P(None, ("dp", "mp"), None),
            P(None, ("dp", "mp"), None),
            P(None, None, "dp", "mp"),
            P(None, "mp", "dp"),
            P(None, "dp", "mp"),
            P(None, "mp", "dp"),
            P(None, None, "dp"),
            P(None, None, "mp", "dp"),
            P(None, "mp", "dp"),
        ),
        check_vma=False,
    )
```

profile of v0, /device:TPU:0, one launch (start us, length us, event | category | flops | bytes accessed | tf_op | source)
XLA Modules:
  0.0 2838.2 jit_solution(727806603229941427)
XLA Ops:
  14.1 2135.3 %while.44 = (s32[]{:T(128)}, f32[3,1024,512]{1,2,0:T(8,128)}, f32[512,1024]{1,0:T(8,128)}, f32[1024,2048]{1,0:T(8,128)}, f32[2048,1024]{1,0:T(8,128)}, /*index=5...) while((s32[]{:T(128)}, f32[3,1024,512]{1,2,0:T(8,128)}, ...), condition=%wide.region_53.54_spmd.clone, body=%wide.region_0.53_spmd.clone.sunk | while | flops 51434610688 | bytes 1139484800 | solution.py:349
  92.7 44.7 %all-gather.107.cloned.1.call-done = bf16[1,3,1024,512]{3,2,1,0:T(8,128)(2,1)} async-done(((bf16[1,3,64,512]{3,2,1,0:T(8,128)(2,1)}), bf16[1,3,1024,512]{3,2,1,0:T(8,128)(2,1)}) %all-gather.107.cloned.1.call-update) | async-done | bytes 3145744 | tf_op jit(solution)/shard_map/while/body/eval_jaxpr/all_gather | solution.py:313
  292.3 44.5 %all-gather.115.cloned.1.call-done = bf16[1,2048,1024]{1,2,0:T(8,128)(2,1)} async-done(((bf16[1,2048,64]{1,2,0:T(8,128)(2,1)}), bf16[1,2048,1024]{1,2,0:T(8,128)(2,1)}) %all-gather.115.cloned.1.call-update) | async-done | bytes 4194320 | tf_op jit(solution)/shard_map/while/body/eval_jaxpr/all_gather | solution.py:316
  424.6 45.3 %all-gather.119.cloned.1.call-done = bf16[1,3,1024,512]{3,2,1,0:T(8,128)(2,1)} async-done(((bf16[1,3,64,512]{3,2,1,0:T(8,128)(2,1)}), bf16[1,3,1024,512]{3,2,1,0:T(8,128)(2,1)}) %all-gather.119.cloned.1.call-update) | async-done | bytes 3145744 | tf_op jit(solution)/shard_map/while/body/eval_jaxpr/all_gather | solution.py:313
  512.3 34.3 %fusion.429 = bf16[312,1024]{1,0:T(8,128)(2,1)S(1)} fusion(bf16[616,1024]{1,0:T(8,128)(2,1)} %convolution_convert_fusion.15), kind=kCustom, calls=%all-reduce-scatter.2.clone.1 | all-reduce-scatter fusion | flops 638977 | bytes 1901056 | tf_op jit(solution)/shard_map/while
  587.9 46.2 %all-gather.125.cloned.1.call-done = bf16[1,1024,2048]{2,1,0:T(8,128)(2,1)} async-done(((bf16[1,64,2048]{2,1,0:T(8,128)(2,1)}), bf16[1,1024,2048]{2,1,0:T(8,128)(2,1)}) %all-gather.125.cloned.1.call-update) | async-done | bytes 4194320 | tf_op jit(solution)/shard_map/while/body/eval_jaxpr/all_gather | solution.py:315
  641.2 44.1 %all-gather.129.cloned.1.call-done = bf16[1,2048,1024]{1,2,0:T(8,128)(2,1)} async-done(((bf16[1,2048,64]{1,2,0:T(8,128)(2,1)}), bf16[1,2048,1024]{1,2,0:T(8,128)(2,1)}) %all-gather.129.cloned.1.call-update) | async-done | bytes 4194320 | tf_op jit(solution)/shard_map/while/body/eval_jaxpr/all_gather | solution.py:334
  997.3 33.8 %fusion.451 = (bf16[312,1024]{1,0:T(8,128)(2,1)S(1)}, bf16[312,1024]{1,0:T(8,128)(2,1)}) fusion(bf16[616,1024]{1,0:T(8,128)(2,1)} %bitcast_convert_fusion.5, bf16[616,1024]{1,0:T(8,128)(2,1)} %fusion.450), kind=kCustom, calls=%all-reduce-scatter.8.clone.1 | all-reduce-scatter fusion | flops 1277953 | bytes 3801600 | tf_op jit(solution)/shard_map/while
  1155.3 43.5 %all-gather.107.cloned.1.call-done = bf16[1,3,1024,512]{3,2,1,0:T(8,128)(2,1)} async-done(((bf16[1,3,64,512]{3,2,1,0:T(8,128)(2,1)}), bf16[1,3,1024,512]{3,2,1,0:T(8,128)(2,1)}) %all-gather.107.cloned.1.call-update) | async-done | bytes 3145744 | tf_op jit(solution)/shard_map/while/body/eval_jaxpr/all_gather | solution.py:313
  1354.1 44.7 %all-gather.115.cloned.1.call-done = bf16[1,2048,1024]{1,2,0:T(8,128)(2,1)} async-done(((bf16[1,2048,64]{1,2,0:T(8,128)(2,1)}), bf16[1,2048,1024]{1,2,0:T(8,128)(2,1)}) %all-gather.115.cloned.1.call-update) | async-done | bytes 4194320 | tf_op jit(solution)/shard_map/while/body/eval_jaxpr/all_gather | solution.py:316
  1486.4 45.3 %all-gather.119.cloned.1.call-done = bf16[1,3,1024,512]{3,2,1,0:T(8,128)(2,1)} async-done(((bf16[1,3,64,512]{3,2,1,0:T(8,128)(2,1)}), bf16[1,3,1024,512]{3,2,1,0:T(8,128)(2,1)}) %all-gather.119.cloned.1.call-update) | async-done | bytes 3145744 | tf_op jit(solution)/shard_map/while/body/eval_jaxpr/all_gather | solution.py:313
  1574.0 34.3 %fusion.429 = bf16[312,1024]{1,0:T(8,128)(2,1)S(1)} fusion(bf16[616,1024]{1,0:T(8,128)(2,1)} %convolution_convert_fusion.15), kind=kCustom, calls=%all-reduce-scatter.2.clone.1 | all-reduce-scatter fusion | flops 638977 | bytes 1901056 | tf_op jit(solution)/shard_map/while
  1649.8 46.2 %all-gather.125.cloned.1.call-done = bf16[1,1024,2048]{2,1,0:T(8,128)(2,1)} async-done(((bf16[1,64,2048]{2,1,0:T(8,128)(2,1)}), bf16[1,1024,2048]{2,1,0:T(8,128)(2,1)}) %all-gather.125.cloned.1.call-update) | async-done | bytes 4194320 | tf_op jit(solution)/shard_map/while/body/eval_jaxpr/all_gather | solution.py:315
  1703.1 44.1 %all-gather.129.cloned.1.call-done = bf16[1,2048,1024]{1,2,0:T(8,128)(2,1)} async-done(((bf16[1,2048,64]{1,2,0:T(8,128)(2,1)}), bf16[1,2048,1024]{1,2,0:T(8,128)(2,1)}) %all-gather.129.cloned.1.call-update) | async-done | bytes 4194320 | tf_op jit(solution)/shard_map/while/body/eval_jaxpr/all_gather | solution.py:334
  2061.6 33.8 %fusion.451 = (bf16[312,1024]{1,0:T(8,128)(2,1)S(1)}, bf16[312,1024]{1,0:T(8,128)(2,1)}) fusion(bf16[616,1024]{1,0:T(8,128)(2,1)} %bitcast_convert_fusion.5, bf16[616,1024]{1,0:T(8,128)(2,1)} %fusion.450), kind=kCustom, calls=%all-reduce-scatter.8.clone.1 | all-reduce-scatter fusion | flops 1277953 | bytes 3801600 | tf_op jit(solution)/shard_map/while
  2197.2 61.0 %all-reduce.20 = (bf16[2,8,64]{1,0,2:T(2,128)(2,1)S(1)}, bf16[2,8,64]{1,0,2:T(2,128)(2,1)S(1)}, bf16[32,64]{1,0:T(8,128)(2,1)S(1)}, bf16[32,64]{1,0:T(8,128)(2,1)S(1)}) all-reduce(bf16[2,8,64]{1,0,2:T(2,128)(2,1)S(1)} %copy.236, bf16[2,8,64]{1,0,2:T(2,128)(2,1)S(1)} %copy.234, ...), channel_id=35, replica_groups=mesh['dp'=16,'mp'=2] {'dp'}, use_global_device_ids=true, to_apply=%region_66.67.clone | all-reduce | flops 6144 | bytes 24576
  2274.2 54.1 %reduce-scatter.37.cloned.1.call-done = bf16[512,64]{0,1:T(8,128)(2,1)} async-done(((bf16[512,1024]{0,1:T(8,128)(2,1)}), bf16[512,64]{0,1:T(8,128)(2,1)}) %reduce-scatter.37.cloned.1.call-update) | async-done | bytes 65552 | tf_op jit(solution)/shard_map/reduce_scatter | solution.py:357
  2328.3 61.1 %reduce-scatter.39.cloned.1.call-done = bf16[512,64]{0,1:T(8,128)(2,1)} async-done(((bf16[512,1024]{0,1:T(8,128)(2,1)}), bf16[512,64]{0,1:T(8,128)(2,1)}) %reduce-scatter.39.cloned.1.call-update) | async-done | bytes 65552 | tf_op jit(solution)/shard_map/reduce_scatter | solution.py:357
  2391.0 67.4 %reduce-scatter.33.cloned.1.call-done = bf16[3,64,512]{2,1,0:T(8,128)(2,1)} async-done(((bf16[3,1024,512]{2,1,0:T(8,128)(2,1)}), bf16[3,64,512]{2,1,0:T(8,128)(2,1)}) %reduce-scatter.33.cloned.1.call-update) | async-done | bytes 196624 | tf_op jit(solution)/shard_map/reduce_scatter | solution.py:354
  2458.4 68.8 %reduce-scatter.35.cloned.1.call-done = bf16[3,64,512]{2,1,0:T(8,128)(2,1)} async-done(((bf16[3,1024,512]{2,1,0:T(8,128)(2,1)}), bf16[3,64,512]{2,1,0:T(8,128)(2,1)}) %reduce-scatter.35.cloned.1.call-update) | async-done | bytes 196624 | tf_op jit(solution)/shard_map/reduce_scatter | solution.py:354
  2529.1 73.1 %reduce-scatter.41.cloned.1.call-done = bf16[64,2048]{1,0:T(8,128)(2,1)} async-done(((bf16[1024,2048]{1,0:T(8,128)(2,1)}), bf16[64,2048]{1,0:T(8,128)(2,1)}) %reduce-scatter.41.cloned.1.call-update) | async-done | bytes 262160 | tf_op jit(solution)/shard_map/reduce_scatter | solution.py:360
  2602.2 75.6 %reduce-scatter.43.cloned.1.call-done = bf16[64,2048]{1,0:T(8,128)(2,1)} async-done(((bf16[1024,2048]{1,0:T(8,128)(2,1)}), bf16[64,2048]{1,0:T(8,128)(2,1)}) %reduce-scatter.43.cloned.1.call-update) | async-done | bytes 262160 | tf_op jit(solution)/shard_map/reduce_scatter | solution.py:360
  2679.9 73.4 %reduce-scatter.45.cloned.1.call-done = bf16[2048,64]{0,1:T(8,128)(2,1)} async-done(((bf16[2048,1024]{0,1:T(8,128)(2,1)}), bf16[2048,64]{0,1:T(8,128)(2,1)}) %reduce-scatter.45.cloned.1.call-update) | async-done | bytes 262160 | tf_op jit(solution)/shard_map/reduce_scatter | solution.py:363
  2753.3 75.4 %reduce-scatter.47.cloned.1.call-done = bf16[2048,64]{0,1:T(8,128)(2,1)} async-done(((bf16[2048,1024]{0,1:T(8,128)(2,1)}), bf16[2048,64]{0,1:T(8,128)(2,1)}) %reduce-scatter.47.cloned.1.call-update) | async-done | bytes 262160 | tf_op jit(solution)/shard_map/reduce_scatter | solution.py:363
  (957 shorter events, 1616.9 us)
Async XLA Ops:
  70.6 179.0 %all-gather.111.cloned.1.call-start = ((), (), s32[]{:S(2)}) async-start(), calls=%async_computation.23 | async-start | bytes 1916928 | tf_op jit(solution)/shard_map/while/body/eval_jaxpr/all_gather | solution.py:42
  209.3 127.5 %all-gather.115.cloned.1.call-start = ((), (), s32[]{:S(2)}) async-start(), calls=%async_computation.25 | async-start | bytes 4456448 | tf_op jit(solution)/shard_map/while/body/eval_jaxpr/all_gather | solution.py:316
  210.3 212.7 %all-gather.117.cloned.1.call-start = ((), (), s32[]{:S(2)}) async-start(), calls=%async_computation.26 | async-start | bytes 1916928 | tf_op jit(solution)/shard_map/while/body/eval_jaxpr/all_gather | solution.py:42
  402.4 177.7 %all-gather.127.cloned.1.call-start = ((), (), s32[]{:S(2)}) async-start(), calls=%async_computation.31 | async-start | bytes 1916928 | tf_op jit(solution)/shard_map/while/body/eval_jaxpr/all_gather | solution.py:46
  403.5 181.8 %all-gather.123.cloned.1.call-start = ((), (), s32[]{:S(2)}) async-start(), calls=%async_computation.29 | async-start | bytes 1916928 | tf_op jit(solution)/shard_map/while/body/eval_jaxpr/all_gather | solution.py:42
  558.1 127.3 %all-gather.129.cloned.1.call-start = ((), (), s32[]{:S(2)}) async-start(), calls=%async_computation.32 | async-start | bytes 4456448 | tf_op jit(solution)/shard_map/while/body/eval_jaxpr/all_gather | solution.py:334
  558.8 205.3 %all-gather.131.cloned.1.call-start = ((), (), s32[]{:S(2)}) async-start(), calls=%async_computation.33 | async-start | bytes 1916928 | tf_op jit(solution)/shard_map/while/body/eval_jaxpr/all_gather | solution.py:46
  742.5 132.7 %all-gather.133.cloned.1.call-start = ((), (), s32[]{:S(2)}) async-start(), calls=%async_computation.34 | async-start | bytes 1916928 | tf_op jit(solution)/shard_map/while/body/eval_jaxpr/all_gather | solution.py:46
  1133.3 177.5 %all-gather.111.cloned.1.call-start = ((), (), s32[]{:S(2)}) async-start(), calls=%async_computation.23 | async-start | bytes 1916928 | tf_op jit(solution)/shard_map/while/body/eval_jaxpr/all_gather | solution.py:42
  1270.5 128.2 %all-gather.115.cloned.1.call-start = ((), (), s32[]{:S(2)}) async-start(), calls=%async_computation.25 | async-start | bytes 4456448 | tf_op jit(solution)/shard_map/while/body/eval_jaxpr/all_gather | solution.py:316
  1271.5 213.3 %all-gather.117.cloned.1.call-start = ((), (), s32[]{:S(2)}) async-start(), calls=%async_computation.26 | async-start | bytes 1916928 | tf_op jit(solution)/shard_map/while/body/eval_jaxpr/all_gather | solution.py:42
  1464.1 177.8 %all-gather.127.cloned.1.call-start = ((), (), s32[]{:S(2)}) async-start(), calls=%async_computation.31 | async-start | bytes 1916928 | tf_op jit(solution)/shard_map/while/body/eval_jaxpr/all_gather | solution.py:46
  1465.2 182.0 %all-gather.123.cloned.1.call-start = ((), (), s32[]{:S(2)}) async-start(), calls=%async_computation.29 | async-start | bytes 1916928 | tf_op jit(solution)/shard_map/while/body/eval_jaxpr/all_gather | solution.py:42
  1620.0 127.3 %all-gather.129.cloned.1.call-start = ((), (), s32[]{:S(2)}) async-start(), calls=%async_computation.32 | async-start | bytes 4456448 | tf_op jit(solution)/shard_map/while/body/eval_jaxpr/all_gather | solution.py:334
  1620.7 207.8 %all-gather.131.cloned.1.call-start = ((), (), s32[]{:S(2)}) async-start(), calls=%async_computation.33 | async-start | bytes 1916928 | tf_op jit(solution)/shard_map/while/body/eval_jaxpr/all_gather | solution.py:46
  1806.9 132.7 %all-gather.133.cloned.1.call-start = ((), (), s32[]{:S(2)}) async-start(), calls=%async_computation.34 | async-start | bytes 1916928 | tf_op jit(solution)/shard_map/while/body/eval_jaxpr/all_gather | solution.py:46
  2152.8 175.5 %reduce-scatter.37.cloned.1.call-start = ((), (), s32[]{:S(2)}) async-start(), calls=%async_computation.12 | async-start | bytes 1114112 | tf_op jit(solution)/shard_map/reduce_scatter | solution.py:357
  2155.5 233.8 %reduce-scatter.39.cloned.1.call-start = ((), (), s32[]{:S(2)}) async-start(), calls=%async_computation.13 | async-start | bytes 1114112 | tf_op jit(solution)/shard_map/reduce_scatter | solution.py:357
  2157.0 301.4 %reduce-scatter.33.cloned.1.call-start = ((), (), s32[]{:S(2)}) async-start(), calls=%async_computation.10 | async-start | bytes 3342336 | tf_op jit(solution)/shard_map/reduce_scatter | solution.py:354
  2162.5 364.6 %reduce-scatter.35.cloned.1.call-start = ((), (), s32[]{:S(2)}) async-start(), calls=%async_computation.11 | async-start | bytes 3342336 | tf_op jit(solution)/shard_map/reduce_scatter | solution.py:354
  2168.0 434.2 %reduce-scatter.41.cloned.1.call-start = ((), (), s32[]{:S(2)}) async-start(), calls=%async_computation.14 | async-start | bytes 4456448 | tf_op jit(solution)/shard_map/reduce_scatter | solution.py:360
  2174.1 503.7 %reduce-scatter.43.cloned.1.call-start = ((), (), s32[]{:S(2)}) async-start(), calls=%async_computation.15 | async-start | bytes 4456448 | tf_op jit(solution)/shard_map/reduce_scatter | solution.py:360
  2180.2 573.1 %reduce-scatter.45.cloned.1.call-start = ((), (), s32[]{:S(2)}) async-start(), calls=%async_computation.16 | async-start | bytes 4456448 | tf_op jit(solution)/shard_map/reduce_scatter | solution.py:363
  2187.6 641.1 %reduce-scatter.47.cloned.1.call-start = ((), (), s32[]{:S(2)}) async-start(), calls=%async_computation.17 | async-start | bytes 4456448 | tf_op jit(solution)/shard_map/reduce_scatter | solution.py:363
  (226 other events, 5142.7 us)
Sparse Core Ops, SparseCore 0:
  92.1 45.2 all-gather.106
  140.1 36.7 all-gather.108
  234.3 50.8 all-gather.112
  287.8 49.0 all-gather.114
  424.7 45.2 all-gather.118
  472.1 36.7 all-gather.120
  510.3 36.2 all-gather.126
  557.6 23.2 all-gather.122
  583.5 50.5 all-gather.124
  636.3 49.0 all-gather.128
  849.6 25.5 all-gather.132
  923.5 25.5 all-gather.134
  1153.5 45.2 all-gather.106
  1201.5 36.7 all-gather.108
  1269.7 23.2 all-gather.110
  1295.8 51.0 all-gather.112
  1349.7 49.0 all-gather.114
  1486.4 45.2 all-gather.118
  1533.9 36.7 all-gather.120
  1572.0 36.2 all-gather.126
  1645.4 50.5 all-gather.124
  1698.2 49.0 all-gather.128
  1913.9 25.5 all-gather.132
  1987.8 25.5 all-gather.134
  (8 shorter events, 173.0 us)
Sparse Core Ops, SparseCore 1:
  2153.9 55.4 reduce-scatter.50
  2213.4 54.3 reduce-scatter.48
  2271.9 56.4 reduce-scatter.36
  2332.9 56.4 reduce-scatter.38
  2393.2 65.1 reduce-scatter.32
  2462.2 64.9 reduce-scatter.34
  2530.9 71.3 reduce-scatter.40
  2606.4 71.3 reduce-scatter.42
  2681.6 71.7 reduce-scatter.44
  2757.7 71.0 reduce-scatter.46
where the time goes:
time: 2850 us; the launch traced here: 2840 us
  waiting for transfers between devices  1190 us (42%)
  blocking collectives  640 us (22%)
  matrix products  422 us (15%)
  local copies, waits for them, and re-layouts  394 us (14%)
  other arithmetic  125 us (4%)
  starting transfers between devices  44.1 us (2%)
    while x14, blocking collectives  339 us
    all_gather x4, waiting for transfers between devices, one_micro(): lax.all_gather(qkv_weight[layer], 'dp', axis=1, tiled=True)  179 us
    all_gather x4, waiting for transfers between devices, one_micro(): lax.all_gather(down_weight[layer], 'dp', axis=1, tiled=True)  177 us
    all_gather x4, waiting for transfers between devices, one_micro(): lax.all_gather(up_weight[layer], 'dp', axis=0, tiled=True)  159 us
    reduce_scatter x2, waiting for transfers between devices, on_device(): lax.psum_scatter(totals[3].astype(jnp.bfloat16), 'dp', scatter_dimension=...  149 us
    reduce_scatter x2, waiting for transfers between devices, on_device(): lax.psum_scatter(totals[2].astype(jnp.bfloat16), 'dp', scatter_dimension=...  149 us
    while x418, local copies, waits for them, and re-layouts  137 us
    reduce_scatter x2, waiting for transfers between devices, on_device(): lax.psum_scatter(totals[0].astype(jnp.bfloat16), 'dp', scatter_dimension=...  136 us
  transfers between devices with their start and end apart: 58, of which 37 were waited for; matrix products, arithmetic and copies ran while one was open for 18% of the time, Pallas kernels for 0%

commit v1 on v0

--- a/solution.py
+++ b/solution.py
@@ -1,8 +1,11 @@
+import functools
 import math
 
 import jax
 import jax.numpy as jnp
 from jax import lax
+from jax.experimental import pallas as pl
+from jax.experimental.pallas import tpu as pltpu
 from jax.sharding import PartitionSpec as P
 
 INV_ROOT_TWO = 0.7071067811865476
@@ -391,6 +394,831 @@
     )
 
 
+MESH = pl.DeviceIdType.MESH
+NZ, NY, NC, NX = 4, 2, 2, 2
+SHARD = 64
+COLS = 6144
+CHUNK = 1024
+PER_LAYER = COLS // CHUNK
+ROUTES = (("zxy", 0, 16, 0, 1024), ("yzx", 16, 48, 0, 512), ("xzy", 16, 48, 512, 512))
+LAG = 2
+
+
+class Place:
+    def __init__(self):
+        dp = lax.axis_index("dp")
+        self.x = lax.axis_index("mp")
+        self.z = dp // 4
+        self.y = lax.rem(dp // 2, 2)
+        self.c = lax.rem(dp, 2)
+
+    def device(self, x=None, z=None, y=None, c=None):
+        x = self.x if x is None else x
+        z = self.z if z is None else z
+        y = self.y if y is None else y
+        c = self.c if c is None else c
+        return (z * 4 + y * 2 + c, x)
+
+    def other(self, axis):
+        if axis == "x":
+            return self.device(x=1 - self.x)
+        if axis == "y":
+            return self.device(y=1 - self.y)
+        return self.device(c=1 - self.c)
+
+    def along(self, k):
+        return lax.rem(self.z + k, NZ)
+
+
+def greet(place):
+    barrier = pltpu.get_barrier_semaphore()
+    for axis in "cxy":
+        pl.semaphore_signal(barrier, inc=1, device_id=place.other(axis), device_id_type=MESH)
+    for k in (1, 2, 3):
+        pl.semaphore_signal(
+            barrier, inc=1, device_id=place.device(z=place.along(k)), device_id_type=MESH
+        )
+    pl.semaphore_wait(barrier, 6)
+
+
+def block(place, filled, z=None):
+    return (
+        slice(None) if "x" in filled else place.x,
+        slice(None) if "z" in filled else (place.z if z is None else z),
+        slice(None) if "y" in filled else place.y,
+        place.c,
+    )
+
+
+class Spread:
+    def __init__(self, place, axis, source, target, send, recv, base):
+        self.place, self.axis = place, axis
+        self.source, self.target = source, target
+        self.send, self.recv, self.base = send, recv, base
+
+    def single(self):
+        return pltpu.make_async_remote_copy(
+            src_ref=self.source, dst_ref=self.target(None),
+            send_sem=self.send(self.base), recv_sem=self.recv(self.base),
+            device_id=self.place.other(self.axis), device_id_type=MESH)
+
+    def direct(self, k):
+        place = self.place
+        return pltpu.make_async_remote_copy(
+            src_ref=self.source, dst_ref=self.target(None),
+            send_sem=self.send(self.base + k), recv_sem=self.recv(self.base + place.z),
+            device_id=place.device(z=place.along(k)), device_id_type=MESH)
+
+    def arrival(self, z):
+        place = self.place
+        return pltpu.make_async_remote_copy(
+            src_ref=self.source, dst_ref=self.target(z),
+            send_sem=self.send(self.base), recv_sem=self.recv(self.base + z),
+            device_id=place.device(z=z), device_id_type=MESH)
+
+    def passed(self):
+        place = self.place
+        origin = jnp.where(place.z == 2, 0, 3)
+        return origin, pltpu.make_async_remote_copy(
+            src_ref=self.target(origin), dst_ref=self.target(origin),
+            send_sem=self.send(self.base), recv_sem=self.recv(self.base + origin),
+            device_id=place.device(z=3 - origin), device_id_type=MESH)
+
+    def start(self):
+        if self.axis != "z":
+            self.single().start()
+            return
+        for k in (1, 2, 3):
+            if k == 2:
+                self.direct(k).start()
+            else:
+                @pl.when(self.place.z != (3 if k == 1 else 0))
+                def _():
+                    self.direct(k).start()
+
+    def relay(self):
+        if self.axis != "z":
+            return
+
+        @pl.when((self.place.z == 1) | (self.place.z == 2))
+        def _():
+            origin, copy = self.passed()
+            self.arrival(origin).wait_recv()
+            copy.start()
+
+    def arrive(self):
+        if self.axis != "z":
+            self.single().wait_recv()
+            return
+        z = self.place.z
+        inner = (z == 1) | (z == 2)
+        far = jnp.where(z == 2, 0, 3)
+        for k in (1, 2, 3):
+            origin = lax.rem(z + k, NZ)
+
+            @pl.when(jnp.logical_not(inner & (origin == far)))
+            def _():
+                self.arrival(origin).wait_recv()
+
+    def finish(self):
+        if self.axis != "z":
+            self.single().wait_send()
+            return
+        for k in (1, 2, 3):
+            if k == 2:
+                self.direct(k).wait_send()
+            else:
+                @pl.when(self.place.z != (3 if k == 1 else 0))
+                def _():
+                    self.direct(k).wait_send()
+
+        @pl.when((self.place.z == 1) | (self.place.z == 2))
+        def _():
+            self.passed()[1].wait_send()
+
+
+class Gather:
+    def __init__(self, place, chunks, shard, whole, send, recv, sib, local):
+        self.place, self.chunks = place, chunks
+        self.shard, self.whole = shard, whole
+        self.send, self.recv, self.sib, self.local = send, recv, sib, local
+
+    def spot(self, step):
+        return step // PER_LAYER, lax.rem(step, PER_LAYER) * CHUNK
+
+    def spread(self, step, route, phase):
+        order, row, rows, col, cols = ROUTES[route]
+        layer, first = self.spot(step)
+        area = (pl.ds(row, rows), pl.ds(pl.multiple_of(first + col, 128), cols))
+        filled = order[:phase]
+        target = lambda z: self.whole.at[(layer,) + block(self.place, filled, z) + area]
+        source = self.shard.at[(layer,) + area] if phase == 0 else target(None)
+        axis = order[phase]
+        base = {"z": 0, "y": 4, "x": 5}[axis]
+        return Spread(
+            self.place, axis, source, target,
+            lambda slot: self.send.at[step, route, slot], lambda slot: self.recv.at[step, route, slot], base)
+
+    def own(self, step):
+        layer, first = self.spot(step)
+        cols = pl.ds(pl.multiple_of(first, CHUNK), CHUNK)
+        return pltpu.make_async_copy(
+            self.shard.at[layer, :, cols],
+            self.whole.at[(layer,) + block(self.place, "") + (slice(None), cols)], self.local.at[step])
+
+    def sibling(self, step):
+        layer, first = self.spot(step)
+        cols = pl.ds(pl.multiple_of(first, CHUNK), CHUNK)
+        part = self.whole.at[(layer,) + block(self.place, "xyz") + (slice(None), cols)]
+        return pltpu.make_async_remote_copy(
+            src_ref=part, dst_ref=part, send_sem=self.sib.at[0, step], recv_sem=self.sib.at[1, step],
+            device_id=self.place.other("c"), device_id_type=MESH)
+
+    def phase(self, step, number):
+        every = range(len(ROUTES))
+        if number == 0:
+            self.own(step).start()
+        if number == 1:
+            self.own(step).wait()
+        for route in every:
+            if 1 <= number <= 3:
+                self.spread(step, route, number - 1).arrive()
+            if number <= 2:
+                self.spread(step, route, number).start()
+        if number == 3:
+            self.sibling(step).start()
+        if number == 4:
+            self.sibling(step).wait()
+            for route in every:
+                for phase in range(3):
+                    self.spread(step, route, phase).finish()
+
+    def tick(self, step):
+        for number in range(5):
+            at = step - LAG * number
+
+            @pl.when((at >= 0) & (at < self.chunks))
+            def _():
+                self.phase(at, number)
+            if number < 3:
+                early = step - LAG * number - 1
+
+                @pl.when((early >= 0) & (early < self.chunks))
+                def _():
+                    for route in range(len(ROUTES)):
+                        self.spread(early, route, number).relay()
+
+    @property
+    def ticks(self):
+        return self.chunks + 4 * LAG
+
+
+def ag_kernel(chunks, shard, small, tokens, cotangent, whole, small_all, mine, mine_grad, send, recv, sib, local, odd):
+    place = Place()
+    greet(place)
+    gather = Gather(place, chunks, shard, whole, send, recv, sib, local)
+
+    def halves(n, source, target):
+        return (
+            pltpu.make_async_remote_copy(
+                src_ref=source.at[1 - place.x], dst_ref=target.at[place.x],
+                send_sem=odd.at[4 * n], recv_sem=odd.at[4 * n + 1],
+                device_id=place.other("x"), device_id_type=MESH),
+            pltpu.make_async_copy(source.at[place.x], target.at[place.x], odd.at[4 * n + 2]),
+        )
+
+    order = "zyx"
+
+    def small_spread(phase):
+        target = lambda z: small_all.at[block(place, order[:phase], z)]
+        base = {"z": 0, "y": 4, "x": 5}[order[phase]]
+        return Spread(
+            place, order[phase], small if phase == 0 else target(None), target,
+            lambda slot: odd.at[8 + slot], lambda slot: odd.at[16 + slot], base)
+
+    part = small_all.at[block(place, "xyz")]
+    small_sibling = pltpu.make_async_remote_copy(
+        src_ref=part, dst_ref=part, send_sem=odd.at[24], recv_sem=odd.at[25],
+        device_id=place.other("c"), device_id_type=MESH)
+    small_own = pltpu.make_async_copy(small, small_all.at[block(place, "")], odd.at[26])
+    token_copies = halves(0, tokens, mine)
+    grad_copies = halves(1, cotangent, mine_grad)
+    for copy in token_copies:
+        copy.start()
+    small_own.start()
+    small_spread(0).start()
+
+    def tick(step, carry):
+        @pl.when(step == 1)
+        def _():
+            small_spread(0).relay()
+            small_own.wait()
+
+        for phase in (1, 2):
+            @pl.when(step == 1 + phase)
+            def _():
+                small_spread(phase - 1).arrive()
+                small_spread(phase).start()
+
+        @pl.when(step == 4)
+        def _():
+            small_spread(2).arrive()
+            small_sibling.start()
+        gather.tick(step)
+
+        @pl.when(step == chunks // 2)
+        def _():
+            for copy in grad_copies:
+                copy.start()
+        return carry
+
+    lax.fori_loop(0, gather.ticks, tick, 0)
+    small_sibling.wait()
+    for phase in range(3):
+        small_spread(phase).finish()
+    for copy in token_copies + grad_copies:
+        copy.wait()
+
+
+def gather_all(shard, small, tokens, cotangent):
+    layers = shard.shape[0]
+    chunks = layers * PER_LAYER
+    half = tokens.shape
+    any_spec = pl.BlockSpec(memory_space=pl.ANY)
+    return pl.pallas_call(
+        functools.partial(ag_kernel, chunks),
+        out_shape=(
+            jax.ShapeDtypeStruct((layers, NX, NZ, NY, NC, SHARD, COLS), jnp.bfloat16),
+            jax.ShapeDtypeStruct((NX, NZ, NY, NC) + small.shape, small.dtype),
+            jax.ShapeDtypeStruct(half, jnp.bfloat16),
+            jax.ShapeDtypeStruct(half, jnp.bfloat16),
+        ),
+        in_specs=[pl.BlockSpec(memory_space=pltpu.VMEM)] * 4,
+        out_specs=(any_spec,) * 4,
+        scratch_shapes=[
+            pltpu.SemaphoreType.DMA((chunks, len(ROUTES), 6)),
+            pltpu.SemaphoreType.DMA((chunks, len(ROUTES), 6)),
+            pltpu.SemaphoreType.DMA((2, chunks)),
+            pltpu.SemaphoreType.DMA((chunks,)),
+            pltpu.SemaphoreType.DMA((32,)),
+        ],
+        compiler_params=pltpu.CompilerParams(collective_id=1, has_side_effects=True, vmem_limit_bytes=32 * 1024 * 1024),
+        name="gather_all",
+    )(shard, small, tokens, cotangent)
+SLOTS = 5
+
+
+class Scatter:
+    def __init__(self, place, chunks, grads, summed, acc, near, first, second, third, send, recv, local, free):
+        self.place, self.chunks = place, chunks
+        self.grads, self.summed = grads, summed
+        self.acc, self.near = acc, near
+        self.landing = (first, second, third)
+        self.send, self.recv, self.local, self.free = send, recv, local, free
+
+    def spot(self, step):
+        chunk = self.chunks - 1 - step
+        return chunk // PER_LAYER, pl.multiple_of(lax.rem(chunk, PER_LAYER) * CHUNK, CHUNK)
+
+    def slot(self, step):
+        return lax.rem(step, SLOTS)
+
+    def core_copies(self, step):
+        layer, first = self.spot(step)
+        cols = pl.ds(first, CHUNK)
+        slot = self.slot(step)
+        return (
+            pltpu.make_async_remote_copy(
+                src_ref=self.grads.at[layer, :, :, :, 1 - self.place.c, :, cols], dst_ref=self.near.at[slot],
+                send_sem=self.send.at[step, len(ROUTES), 0], recv_sem=self.recv.at[step, len(ROUTES), 0],
+                device_id=self.place.other("c"), device_id_type=MESH),
+            pltpu.make_async_copy(
+                self.grads.at[layer, :, :, :, self.place.c, :, cols], self.acc.at[slot], self.local.at[step]),
+        )
+
+    def core_add(self, step):
+        slot = self.slot(step)
+
+        def one(n, carry):
+            x, z, y = n // 8, lax.rem(n // 2, 4), lax.rem(n, 2)
+            self.acc[slot, x, z, y] = self.acc[slot, x, z, y] + self.near[slot, x, z, y]
+            return carry
+
+        lax.fori_loop(0, NX * NZ * NY, one, 0)
+
+    def area(self, route):
+        _, row, rows, col, cols = ROUTES[route]
+        return (pl.ds(row, rows), pl.ds(col, cols))
+
+    def index(self, route, phase, over):
+        order = ROUTES[route][0]
+        left = order[:2 - phase]
+        place = self.place
+        picked = []
+        for axis, own in (("x", place.x), ("z", place.z), ("y", place.y)):
+            picked.append(over[axis] if axis in over else (slice(None) if axis in left else own))
+        return tuple(picked)
+
+    def copy(self, step, route, phase, over, device, source_slot, sem):
+        slot = self.slot(step)
+        axis = ROUTES[route][0][2 - phase]
+        land = self.landing[phase][route].at[slot]
+        if axis == "z":
+            land = land.at[source_slot]
+        base = {"z": 0, "y": 4, "x": 5}[axis]
+        return pltpu.make_async_remote_copy(
+            src_ref=self.acc.at[(slot,) + self.index(route, phase, over) + self.area(route)], dst_ref=land,
+            send_sem=self.send.at[step, route, base + sem], recv_sem=self.recv.at[step, route, base + source_slot],
+            device_id=device, device_id_type=MESH)
+
+    def single(self, step, route, phase):
+        axis = ROUTES[route][0][2 - phase]
+        own = self.place.x if axis == "x" else self.place.y
+        return self.copy(step, route, phase, {axis: 1 - own}, self.place.other(axis), 0, 0)
+
+    def along(self, step, route, phase, k):
+        place = self.place
+        z = place.along(k)
+        far = (place.z + z == 3) & ((place.z == 0) | (place.z == 3))
+        via = jnp.where(far, jnp.where(place.z == 0, 1, 2), z)
+        return self.copy(
+            step, route, phase, {"z": z}, place.device(z=via), jnp.where(far, via, place.z), k)
+
+    def arrival(self, step, route, phase, z):
+        return self.copy(step, route, phase, {"z": self.place.z}, self.place.device(z=lax.rem(z + 1, NZ)), z, 1)
+
+    def start(self, step, route, phase):
+        if ROUTES[route][0][2 - phase] != "z":
+            self.single(step, route, phase).start()
+            return
+        z = self.place.z
+        for k in (1, 2, 3):
+            if k == 2:
+                @pl.when((z == 0) | (z == 3))
+                def _():
+                    self.along(step, route, phase, k).start()
+            else:
+                self.along(step, route, phase, k).start()
+
+    def relay(self, step, route, phase):
+        if ROUTES[route][0][2 - phase] != "z":
+            return
+        z = self.place.z
+        slot = self.slot(step)
+
+        @pl.when((z == 1) | (z == 2))
+        def _():
+            self.arrival(step, route, phase, z).wait_recv()
+            far = lax.rem(z + 2, NZ)
+            at = (slot,) + self.index(route, phase, {"z": far}) + self.area(route)
+            self.acc[at] = self.acc[at] + self.landing[phase][route][slot, z]
+            self.along(step, route, phase, 2).start()
+
+    def arrive(self, step, route, phase):
+        slot = self.slot(step)
+        area = self.area(route)
+        axis = ROUTES[route][0][2 - phase]
+        land = self.landing[phase][route]
+        if axis != "z":
+            self.single(step, route, phase).wait_recv()
+            at = self.index(route, phase, {axis: self.place.x if axis == "x" else self.place.y})
+            lead = [n for n, entry in enumerate(at) if isinstance(entry, slice)]
+            extents = [(NX, NZ, NY)[n] for n in lead]
+            total = 1
+            for extent in extents:
+                total *= extent
+
+            def one(n, carry):
+                part = []
+                for extent in reversed(extents):
+                    part.append(lax.rem(n, extent))
+                    n = n // extent
+                part.reverse()
+                full = list(at)
+                for position, value in zip(lead, part):
+                    full[position] = value
+                self.acc[(slot,) + tuple(full) + area] = (
+                    self.acc[(slot,) + tuple(full) + area] + land[(slot,) + tuple(part)])
+                return carry
+
+            if total == 1:
+                one(0, 0)
+            else:
+                lax.fori_loop(0, total, one, 0)
+            return
+        z = self.place.z
+        ends = (z == 0) | (z == 3)
+        at = (slot,) + self.index(route, phase, {"z": z}) + area
+        for k in (1, 2, 3):
+            origin = lax.rem(z + k, NZ)
+
+            @pl.when(jnp.logical_not(ends & (z + origin == 3)))
+            def _():
+                self.arrival(step, route, phase, origin).wait_recv()
+                self.acc[at] = self.acc[at] + land[slot, origin]
+
+    def finish(self, step, route, phase):
+        if ROUTES[route][0][2 - phase] != "z":
+            self.single(step, route, phase).wait_send()
+            return
+        for k in (1, 2, 3):
+            self.along(step, route, phase, k).wait_send()
+
+    def others(self):
+        place = self.place
+        pairs = [(place.other(axis), n, n) for n, axis in enumerate("cxy")]
+        for k in (1, 2, 3):
+            z = place.along(k)
+            pairs.append((place.device(z=z), 3 + place.z, 3 + z))
+        return pairs
+
+    def phase(self, step, number):
+        every = range(len(ROUTES))
+        if number == 0:
+            @pl.when(step >= SLOTS)
+            def _():
+                for _, _, mine in self.others():
+                    pl.semaphore_wait(self.free.at[mine], 1)
+            for copy in self.core_copies(step):
+                copy.start()
+            return
+        if number == 1:
+            remote, own = self.core_copies(step)
+            own.wait()
+            remote.wait_recv()
+            self.core_add(step)
+        for route in every:
+            if number >= 2:
+                self.arrive(step, route, number - 2)
+            if number <= 3:
+                self.start(step, route, number - 1)
+        if number == 4:
+            slot = self.slot(step)
+            layer, first = self.spot(step)
+            place = self.place
+            self.summed[layer, :, pl.ds(first, CHUNK)] = self.acc[slot, place.x, place.z, place.y].astype(jnp.float32)
+            self.core_copies(step)[0].wait_send()
+            for route in every:
+                for phase in range(3):
+                    self.finish(step, route, phase)
+
+            @pl.when(step + SLOTS < self.chunks)
+            def _():
+                for device, there, _ in self.others():
+                    pl.semaphore_signal(self.free.at[there], inc=1, device_id=device, device_id_type=MESH)
+
+    def tick(self, step):
+        for number in (4, 3, 2, 1, 0):
+            at = step - number
+
+            @pl.when((at >= 0) & (at < self.chunks))
+            def _():
+                self.phase(at, number)
+            if number >= 2:
+                pass
+        for number in (1, 2, 3):
+            at = step - number
+
+            @pl.when((at >= 0) & (at < self.chunks))
+            def _():
+                for route in range(len(ROUTES)):
+                    self.relay(at, route, number - 1)
+
+    @property
+    def ticks(self):
+        return self.chunks + 4
+
+
+def landing_shapes():
+    shapes = []
+    for phase in range(3):
+        for order, row, rows, col, cols in ROUTES:
+            left = order[:2 - phase]
+            axis = order[2 - phase]
+            lead = tuple(extent for name, extent in (("x", NX), ("z", NZ), ("y", NY)) if name in left)
+            if axis == "z":
+                lead = (NZ,) + lead
+            shapes.append(pltpu.VMEM((SLOTS,) + lead + (rows, cols), jnp.bfloat16))
+    return shapes
+
+
+def rs_kernel(chunks, grads, small, output, tokens_grad, summed, small_sum, out_rows, grad_rows, *scratch):
+    acc, near = scratch[:2]
+    n = len(ROUTES)
+    lands = scratch[2:2 + 3 * n]
+    small_acc, small_c, small_x, small_y, small_z, send, recv, local, free, odd = scratch[2 + 3 * n:]
+    place = Place()
+    greet(place)
+    scatter = Scatter(place, chunks, grads, summed, acc, near, lands[:n], lands[n:2 * n], lands[2 * n:], send, recv, local, free)
+
+    def halves(n, source, target):
+        return (
+            pltpu.make_async_remote_copy(
+                src_ref=source.at[1 - place.x], dst_ref=target.at[place.x],
+                send_sem=odd.at[4 * n], recv_sem=odd.at[4 * n + 1],
+                device_id=place.other("x"), device_id_type=MESH),
+            pltpu.make_async_copy(source.at[place.x], target.at[place.x], odd.at[4 * n + 2]),
+        )
+
+    def small_copy(source, target, device, base, there=0):
+        return pltpu.make_async_remote_copy(
+            src_ref=source, dst_ref=target, send_sem=odd.at[8 + base], recv_sem=odd.at[16 + there],
+            device_id=device, device_id_type=MESH)
+
+    core = small_copy(small.at[1 - place.c], small_c, place.other("c"), 0, 0)
+    over_x = small_copy(small_acc.at[1 - place.x], small_x, place.other("x"), 1, 1)
+    over_y = small_copy(small_acc.at[place.x, 1 - place.y], small_y, place.other("y"), 2, 2)
+    over_z = [
+        small_copy(small_acc.at[place.x, place.y, place.along(k)], small_z.at[k - 1], place.device(z=place.along(k)), 2 + k, 2 + k)
+        for k in (1, 2, 3)
+    ]
+    rows_copies = halves(0, output, out_rows) + halves(1, tokens_grad, grad_rows)
+    for copy in rows_copies:
+        copy.start()
+    core.start()
+
+    def tick(step, carry):
+        @pl.when(step == 1)
+        def _():
+            core.wait()
+            small_acc[...] = small[place.c] + small_c[...]
+            over_x.start()
+
+        @pl.when(step == 2)
+        def _():
+            over_x.wait()
+            small_acc[place.x] = small_acc[place.x] + small_x[...]
+            over_y.start()
+
+        @pl.when(step == 3)
+        def _():
+            over_y.wait()
+            small_acc[place.x, place.y] = small_acc[place.x, place.y] + small_y[...]
+            for copy in over_z:
+                copy.start()
+        scatter.tick(step)
+        return carry
+
+    lax.fori_loop(0, scatter.ticks, tick, 0)
+    for copy in over_z:
+        copy.wait()
+    small_sum[...] = small_acc[place.x, place.y, place.z] + small_z[0] + small_z[1] + small_z[2]
+    for copy in rows_copies:
+        copy.wait()
+
+
+def scatter_all(grads, small, output, tokens_grad):
+    layers = grads.shape[0]
+    chunks = layers * PER_LAYER
+    any_spec = pl.BlockSpec(memory_space=pl.ANY)
+    vmem = pl.BlockSpec(memory_space=pltpu.VMEM)
+    tail = small.shape[4:]
+    return pl.pallas_call(
+        functools.partial(rs_kernel, chunks),
+        out_shape=(
+            jax.ShapeDtypeStruct((layers, SHARD, COLS), jnp.float32),
+            jax.ShapeDtypeStruct(tail, jnp.float32),
+            jax.ShapeDtypeStruct(output.shape, output.dtype),
+            jax.ShapeDtypeStruct(tokens_grad.shape, tokens_grad.dtype),
+        ),
+        in_specs=[any_spec, vmem, vmem, vmem],
+        out_specs=(vmem, vmem, any_spec, any_spec),
+        scratch_shapes=[
+            pltpu.VMEM((SLOTS, NX, NZ, NY, SHARD, CHUNK), jnp.bfloat16),
+            pltpu.VMEM((SLOTS, NX, NZ, NY, SHARD, CHUNK), jnp.bfloat16),
+        ] + landing_shapes() + [
+            pltpu.VMEM((NX, NY, NZ) + tail, jnp.float32),
+            pltpu.VMEM((NX, NY, NZ) + tail, jnp.float32),
+            pltpu.VMEM((NY, NZ) + tail, jnp.float32),
+            pltpu.VMEM((NZ,) + tail, jnp.float32),
+            pltpu.VMEM((3,) + tail, jnp.float32),
+            pltpu.SemaphoreType.DMA((chunks, len(ROUTES) + 1, 6)),
+            pltpu.SemaphoreType.DMA((chunks, len(ROUTES) + 1, 6)),
+            pltpu.SemaphoreType.DMA((chunks,)),
+            pltpu.SemaphoreType.REGULAR((7,)),
+            pltpu.SemaphoreType.DMA((32,)),
+        ],
+        compiler_params=pltpu.CompilerParams(collective_id=2, has_side_effects=True, vmem_limit_bytes=56 * 1024 * 1024),
+        name="scatter_all",
+    )(grads, small, output, tokens_grad)
+
+
+WINDOWS = ((0, 208), (208, 208), (416, 224))
+PADDED = 640
+HALF_PAD = 320
+
+
+def pack_small(vectors, qv_bias, up_bias):
+    flat = jnp.concatenate([vectors.reshape(-1), qv_bias.reshape(-1), up_bias.reshape(-1)])
+    return jnp.pad(flat, (0, 2048 - flat.shape[0])).reshape(16, 128)
+
+
+def placement(ids):
+    same = ids[:, None] == ids[None, :]
+    count = jnp.sum(same, axis=1)
+    order = jnp.arange(ids.shape[0])
+    before = order[None, :] < order[:, None]
+    long = count > 100
+    kind = (long[:, None] == long[None, :]) & before
+    inside = jnp.sum(same & before, axis=1)
+    earlier = jnp.sum(kind, axis=1) - inside
+    return jnp.where(long, jnp.where(earlier > 0, 208, 0) + inside, 416 + earlier + inside)
+
+
+def on_device_fast(
+    tokens, segments, qkv_weight, out_weight, up_weight, down_weight, vectors, qv_bias, up_bias, cotangent
+):
+    layers = qkv_weight.shape[0]
+    half = tokens.shape[1]
+    width = tokens.shape[2]
+    place_x = lax.axis_index("mp")
+    shard = jnp.concatenate(
+        [qkv_weight[:, 0], qkv_weight[:, 1], qkv_weight[:, 2], jnp.swapaxes(out_weight, 1, 2),
+         up_weight, jnp.swapaxes(down_weight, 1, 2)], axis=2)
+    extra = ((0, 0), (0, HALF_PAD - half), (0, 0))
+    whole, small_all, mine, mine_grad = gather_all(
+        shard, pack_small(vectors, qv_bias, up_bias), jnp.pad(tokens, extra), jnp.pad(cotangent, extra))
+    weights = whole.reshape(layers, 2, width, COLS)
+    small_flat = small_all.reshape(2, 16, 2048).astype(jnp.float32)
+    vector_all = small_flat[0, :, :1024].reshape(16, layers, 8, 64).transpose(1, 2, 0, 3).reshape(layers, 8, width)
+    qv_all = small_flat[:, :, 1024:1152].reshape(2, 16, layers, 2, 8, 4).transpose(2, 3, 0, 4, 1, 5).reshape(layers, 2, width)
+    up_all = small_flat[:, :, 1152:1408].reshape(2, 16, layers, 32, 4).transpose(2, 0, 3, 1, 4).reshape(layers, 4096)
+
+    ids = lax.dynamic_index_in_dim(segments, place_x, 0, keepdims=False)
+    position = placement(ids)
+    spread = jnp.concatenate([
+        jnp.pad(position[:half], (0, HALF_PAD - half), constant_values=-1),
+        jnp.pad(position[half:], (0, HALF_PAD - half), constant_values=-1)])
+    to_place = (jnp.arange(PADDED)[:, None] == spread[None, :]).astype(jnp.bfloat16)
+    new_ids = jnp.max(jnp.where(jnp.arange(PADDED)[:, None] == position[None, :], ids[None, :], -1), axis=1)
+
+    def sort(rows):
+        return jnp.dot(to_place, rows, preferred_element_type=jnp.float32)
+
+    def unsort(rows):
+        return jnp.dot(to_place.T, rows, preferred_element_type=jnp.float32).astype(jnp.bfloat16)
+
+    resid = sort(mine.reshape(PADDED, width))
+    upstream = sort(mine_grad.reshape(PADDED, width))
+    masks = [(new_ids[a:a + n][:, None] == new_ids[a:a + n][None, :])[None] for a, n in WINDOWS]
+    scale = 0.125
+
+    def project(rows, weight):
+        return jnp.einsum("rd,xdc->rxc", rows, weight, preferred_element_type=jnp.float32).reshape(rows.shape[0], -1)
+
+    def project_t(rows, weight):
+        return jnp.einsum("rxi,xoi->ro", rows.reshape(rows.shape[0], 2, -1), weight, preferred_element_type=jnp.float32)
+
+    def heads(rows, a, n):
+        return rows[a:a + n].reshape(n, 16, 64)
+
+    def probabilities(query, keys, w):
+        a, n = WINDOWS[w]
+        raw = jnp.einsum("qhd,khd->hqk", heads(query, a, n), heads(keys, a, n), preferred_element_type=jnp.float32) * scale
+        raw = jnp.where(masks[w], raw, -1e9)
+        powers = jnp.exp(raw - jnp.max(raw, axis=-1, keepdims=True))
+        return powers / jnp.sum(powers, axis=-1, keepdims=True)
+
+    saves = []
+    for layer in range(layers):
+        w = weights[layer]
+        vec = vector_all[layer]
+        normed_in, n1, r1 = layer_norm(resid, vec[0], vec[1])
+        first = normed_in.astype(jnp.bfloat16)
+        query = (project(first, w[:, :, 0:512]) + qv_all[layer, 0]).astype(jnp.bfloat16)
+        keys = project(first, w[:, :, 512:1024]).astype(jnp.bfloat16)
+        values = (project(first, w[:, :, 1024:1536]) + qv_all[layer, 1]).astype(jnp.bfloat16)
+        parts = []
+        for i, (a, n) in enumerate(WINDOWS):
+            probs = probabilities(query, keys, i).astype(jnp.bfloat16)
+            parts.append(jnp.einsum("hqk,khd->qhd", probs, heads(values, a, n), preferred_element_type=jnp.float32).reshape(n, -1))
+        attended = jnp.concatenate(parts).astype(jnp.bfloat16)
+        projected = project_t(attended, w[:, :, 1536:2048])
+        middle = resid + vec[3] * (projected + vec[2])
+        normed_mid, n2, r2 = layer_norm(middle, vec[4], vec[5])
+        second = normed_mid.astype(jnp.bfloat16)
+        pre = project(second, w[:, :, 2048:4096]) + up_all[layer]
+        hidden = (0.5 * pre * (1.0 + lax.erf(pre * INV_ROOT_TWO))).astype(jnp.bfloat16)
+        returned = project_t(hidden, w[:, :, 4096:])
+        resid = middle + vec[7] * (returned + vec[6])
+        saves.append((n1, r1, first, query, keys, values, attended, projected, n2, r2, second, pre, hidden, returned))
+    output = resid.astype(jnp.bfloat16)
+
+    def grad_w(left, right):
+        n = right.shape[1] // 2
+        return jnp.einsum("rd,rxc->xdc", left, right.reshape(-1, 2, n), preferred_element_type=jnp.float32).astype(jnp.bfloat16)
+
+    all_grads = [None] * layers
+    small_grads = [None] * layers
+    for layer in reversed(range(layers)):
+        w = weights[layer]
+        vec = vector_all[layer]
+        n1, r1, first, query, keys, values, attended, projected, n2, r2, second, pre, hidden, returned = saves[layer]
+        scaled_up = vec[7] * upstream
+        g6 = jnp.sum(scaled_up, axis=0)
+        g7 = jnp.sum(upstream * (returned + vec[6]), axis=0)
+        d_returned = scaled_up.astype(jnp.bfloat16)
+        grad_down = grad_w(d_returned, hidden)
+        d_hidden = project(d_returned, w[:, :, 4096:])
+        cdf = 0.5 * (1.0 + lax.erf(pre * INV_ROOT_TWO))
+        pdf = jnp.exp(-0.5 * pre * pre) * INV_ROOT_TAU
+        d_pre = (d_hidden * (cdf + pre * pdf)).astype(jnp.bfloat16)
+        g_up_bias = jnp.sum(d_pre.astype(jnp.float32), axis=0)
+        grad_up = grad_w(second, d_pre)
+        d_second = project_t(d_pre, w[:, :, 2048:4096])
+        d_mid, g4, g5 = norm_backward(d_second, n2, r2, vec[4])
+        d_middle = upstream + d_mid
+        scaled_mid = vec[3] * d_middle
+        g2 = jnp.sum(scaled_mid, axis=0)
+        g3 = jnp.sum(d_middle * (projected + vec[2]), axis=0)
+        d_projected = scaled_mid.astype(jnp.bfloat16)
+        grad_out = grad_w(d_projected, attended)
+        d_attended = project(d_projected, w[:, :, 1536:2048]).astype(jnp.bfloat16)
+        dq, dk, dv = [], [], []
+        for i, (a, n) in enumerate(WINDOWS):
+            p = probabilities(query, keys, i)
+            da = heads(d_attended, a, n)
+            dv.append(jnp.einsum("hqk,qhd->khd", p.astype(jnp.bfloat16), da, preferred_element_type=jnp.float32).reshape(n, -1))
+            dp = jnp.einsum("qhd,khd->hqk", da, heads(values, a, n), preferred_element_type=jnp.float32)
+            ds = (p * (dp - jnp.sum(p * dp, axis=-1, keepdims=True))).astype(jnp.bfloat16)
+            dq.append((jnp.einsum("hqk,khd->qhd", ds, heads(keys, a, n), preferred_element_type=jnp.float32) * scale).reshape(n, -1))
+            dk.append((jnp.einsum("hqk,qhd->khd", ds, heads(query, a, n), preferred_element_type=jnp.float32) * scale).reshape(n, -1))
+        dq, dk, dv = [jnp.concatenate(v).astype(jnp.bfloat16) for v in (dq, dk, dv)]
+        g_qv = jnp.stack([jnp.sum(dq.astype(jnp.float32), axis=0), jnp.sum(dv.astype(jnp.float32), axis=0)])
+        d_first = project_t(dq, w[:, :, 0:512]) + project_t(dk, w[:, :, 512:1024]) + project_t(dv, w[:, :, 1024:1536])
+        d_in, g0, g1 = norm_backward(d_first, n1, r1, vec[0])
+        upstream = d_middle + d_in
+        all_grads[layer] = jnp.concatenate(
+            [grad_w(first, dq), grad_w(first, dk), grad_w(first, dv), grad_out, grad_up, grad_down], axis=2)
+        small_grads[layer] = (jnp.stack([g0, g1, g2, g3, g4, g5, g6, g7]), g_qv, g_up_bias)
+    grads = jnp.stack(all_grads).reshape(layers, NX, NZ, NY, NC, SHARD, COLS)
+    return finish_fast(grads, small_grads, unsort(output), unsort(upstream.astype(jnp.bfloat16)), half)
+
+
+def finish_fast(grads, small_grads, output, tokens_grad, half):
+    layers = grads.shape[0]
+    width = output.shape[1]
+    vec = jnp.stack([s[0] for s in small_grads]).reshape(layers, 8, 16, 64).transpose(2, 0, 1, 3).reshape(1, 16, 1024)
+    qv = jnp.stack([s[1] for s in small_grads]).reshape(layers, 2, 2, 8, 16, 4).transpose(2, 4, 0, 1, 3, 5).reshape(2, 16, 128)
+    ups = jnp.stack([s[2] for s in small_grads]).reshape(layers, 2, 32, 16, 4).transpose(1, 3, 0, 2, 4).reshape(2, 16, 256)
+    small = jnp.concatenate([jnp.broadcast_to(vec, (2, 16, 1024)), qv, ups, jnp.zeros((2, 16, 640), jnp.float32)], axis=2)
+    small = small.reshape(NX, NZ, NY, NC, 16, 128).transpose(3, 0, 2, 1, 4, 5)
+    summed, small_sum, out_rows, grad_rows = scatter_all(
+        grads, small, output.reshape(2, HALF_PAD, width), tokens_grad.reshape(2, HALF_PAD, width))
+    flat = small_sum.reshape(-1)
+    return (
+        out_rows[:, :half],
+        grad_rows[:, :half].astype(jnp.float32),
+        jnp.stack([summed[:, :, 0:512], summed[:, :, 512:1024], summed[:, :, 1024:1536]], axis=1),
+        jnp.swapaxes(summed[:, :, 1536:2048], 1, 2),
+        summed[:, :, 2048:4096],
+        jnp.swapaxes(summed[:, :, 4096:], 1, 2),
+        flat[:1024].reshape(layers, 8, 64),
+        flat[1024:1152].reshape(layers, 2, 8, 4),
+        flat[1152:1408].reshape(layers, 32, 4),
+    )
+
+
 def solution(mesh):
     placed = (
         P(None, ("dp", "mp"), None),
@@ -404,8 +1232,9 @@
         P(None, "mp", "dp"),
         P(None, ("dp", "mp"), None),
     )
+    fast = dict(mesh.shape) == {"dp": NZ * NY * NC, "mp": NX}
     return jax.shard_map(
-        on_device,
+        on_device_fast if fast else on_device,
         mesh=mesh,
         in_specs=placed,
         out_specs=(

time: 2850 us -> 1090 us (0.38)
  waiting for transfers between devices: 1190 us -> 0 us
  blocking collectives: 640 us -> 0 us
  Pallas kernels: 0 us -> 483 us
  local copies, waits for them, and re-layouts: 394 us -> 203 us
  matrix products: 422 us -> 327 us
  other arithmetic: 125 us -> 60.7 us
  starting transfers between devices: 44.1 us -> 0 us
    all_gather x32 -> x0, waiting for transfers between devices: 619 us -> none  [the longest x4 179 us: one_micro(): lax.all_gather(qkv_weight[layer], 'dp', axis=1, tiled=True)]
    reduce_scatter x8 -> x0, waiting for transfers between devices: 549 us -> none  [the longest x2 149 us: on_device(): lax.psum_scatter(totals[3].astype(jnp.bfloat16), 'dp', scatter_dimension=...]
    pallas_call x0 -> x2, Pallas kernels: none -> 483 us  [the longest x1 265 us: scatter_all(): pl.pallas_call(functools.partial(rs_kernel, chunks), out_shape=(jax.Shape...]
    while x14 -> x0, blocking collectives: 339 us -> none
    all_gather x12 -> x0, blocking collectives: 235 us -> none  [the longest x4 85.7 us: one_micro(): lax.all_gather(vectors[layer], 'dp', axis=1, tiled=True)]
    while x424 -> x0, local copies, waits for them, and re-layouts: 167 us -> none
    dot_general x80 -> x70, matrix products: 422 us -> 304 us  [the longest x12 84.4 us: project_t(): jnp.einsum('rxi,xoi->ro', rows.reshape(rows.shape[0], 2, -1), weight, pre...]
    concatenate x0 -> x19, local copies, waits for them, and re-layouts: none -> 90.9 us  [the longest x2 65.8 us: on_device_fast(): jnp.concatenate([grad_w(first, dq), grad_w(first, dk), grad_w(first, dv),...]
  transfers between devices with their start and end apart: 58 -> 0, of which waited for: 37 -> 0; matrix products, arithmetic and copies ran while one was open for 18% -> 0% of each run, Pallas kernels for 0% -> 0%
where the time goes in v1:
time: 1090 us; the launch traced here: 1080 us
  Pallas kernels  483 us (44%)
  matrix products  327 us (30%)
  local copies, waits for them, and re-layouts  203 us (19%)
  other arithmetic  60.7 us (6%)
    pallas_call x1, Pallas kernels, scatter_all(): pl.pallas_call(functools.partial(rs_kernel, chunks), out_shape=(jax.Shape...  265 us
    pallas_call x1, Pallas kernels, gather_all(): pl.pallas_call(functools.partial(ag_kernel, chunks), out_shape=(jax.Shape...  218 us
    dot_general x12, matrix products, project_t(): jnp.einsum('rxi,xoi->ro', rows.reshape(rows.shape[0], 2, -1), weight, pre...  84.4 us
    dot_general x12, matrix products, project(): jnp.einsum('rd,xdc->rxc', rows, weight, preferred_element_type=jnp.float32)  78 us
    dot_general x12, matrix products, grad_w(): jnp.einsum('rd,rxc->xdc', left, right.reshape(-1, 2, n), preferred_elemen...  66.1 us
    concatenate x2, local copies, waits for them, and re-layouts, on_device_fast(): jnp.concatenate([grad_w(first, dq), grad_w(first, dk), grad_w(first, dv),...  65.8 us
    slice x1, local copies, waits for them, and re-layouts, on_device_fast(): w = weights[layer]  34.7 us
    another operation x1, other arithmetic, on_device_fast(): grads = jnp.stack(all_grads).reshape(layers, NX, NZ, NY, NC, SHARD, COLS)  33.8 us

profile of v1, /device:TPU:0, one launch (start us, length us, event | category | flops | bytes accessed | tf_op | source)
XLA Modules:
  0.0 1077.2 jit_solution(12691584843355524155)
XLA Ops:
  11.3 218.4 %gather_all.1 = (bf16[2,2,4,2,2,64,6144]{6,5,4,3,2,1,0:T(8,128)(2,1)}, bf16[2,4,2,2,16,128]{5,4,3,2,1,0:T(8,128)(2,1)S(1)}, bf16[2,320,1024]{2,1,0:T(8,128)(2,1)S(1)}, bf16[2,320,1024]{2,1,0:T(8,128)(2,1)S(1)}) custom-call(bf16[2,64,6144]{2,1,0:T(8,128)(2,1)S(1)} %bitcast_dynamic-update-slice_fusion.12.shard, bf16[16,128]{1,0:T(8,128)(2,1)S(1)} %fusion.194.small, ...), custom_call_target="tpu_custom_call" | custom-call | tf_op jit(solution)/shard_map/gather_all/pallas_call | solution.py:688
  248.5 34.7 %fusion.230 = (bf16[1,2,4,2,2,64,6144]{6,5,4,3,2,1,0:T(8,128)(2,1)}, bf16[1,2,4,2,2,64,6144]{6,5,4,3,2,1,0:T(8,128)(2,1)}) fusion(bf16[2,2,4,2,2,64,6144]{6,5,4,3,2,1,0:T(8,128)(2,1)} %get-tuple-element.19), kind=kLoop, calls=%fused_computation.410 | loop fusion | bytes 100663296 | tf_op jit(solution)/shard_map/slice | solution.py:1124
  325.5 5.1 fusion.229
  331.3 11.7 %multiply_convert_fusion.1 = (bf16[640,2,2048]{2,0,1:T(8,128)(2,1)S(1)}, f32[640,2,2048]{2,0,1:T(8,128)}) fusion(f32[2,2048]{1,0:T(2,128)S(1)} %add.313, bf16[2,1024,6144]{2,1,0:T(8,128)(2,1)} %bitcast.442, f32[640,1024]{1,0:T(8,128)S(1)} %get-tuple-element.111, f32[1024]{0:T(1024)S(1)} %copy-done.171, f32[1024]{0:T(1024)S(1)} %mul.503, ...), kind=kOutput, calls=%fused_computation.25 | convolution fusion | flops 5387714560 | bytes 26768384 | tf_op jit(solution)/shard_map/rd,xdc->rxc/dot_general | solution.py:1107
  343.1 11.3 %fusion.228 = (f32[640]{0:T(1024)S(1)}, f32[640,1024]{1,0:T(8,128)S(1)}, f32[640,1024,1]{1,0,2:T(8,128)}) fusion(f32[640,1024]{1,0:T(8,128)S(1)} %get-tuple-element.111, f32[1024]{0:T(1024)S(1)} %copy-done.147, f32[1024]{0:T(1024)S(1)} %mul.498, bf16[640,2,2048]{2,0,1:T(8,128)(2,1)S(1)} %get-tuple-element.156, bf16[2,1024,6144]{2,1,0:T(8,128)(2,1)} %bitcast.443), kind=kOutput, calls=%fused_computation.408 | convolution fusion | flops 5371330048 | bytes 21506560 | tf_op jit(solution)/shard_map/rxi,xoi->ro/dot_general | solution.py:1110
  403.5 5.1 fusion.227
  409.3 11.1 %multiply_convert_fusion = (bf16[640,2,2048]{2,0,1:T(8,128)(2,1)}, f32[640,2,2048]{2,0,1:T(8,128)S(1)}) fusion(f32[2,2048]{1,0:T(2,128)S(1)} %copy-done.156, bf16[2,1024,6144]{2,1,0:T(8,128)(2,1)} %bitcast.454, f32[640,1024]{1,0:T(8,128)S(1)} %get-tuple-element.107, f32[1024]{0:T(1024)S(1)} %copy-done.169, f32[1024]{0:T(1024)S(1)} %copy-done.165, ...), kind=kOutput, calls=%fused_computation.23 | convolution fusion | flops 5387714560 | bytes 26768384 | tf_op jit(solution)/shard_map/rd,xdc->rxc/dot_general | solution.py:1107
  420.4 11.8 %convert_reduce_fusion = (f32[2,2048]{1,0:T(2,128)S(1)}, bf16[640,2,2048]{2,0,1:T(8,128)(2,1)}) fusion(f32[640,2,2048]{2,0,1:T(8,128)S(1)} %get-tuple-element.167, f32[2,2048]{1,0:T(2,128)S(1)} %copy-done.156, bf16[2,1024,6144]{2,1,0:T(8,128)(2,1)} %bitcast.455, f32[640,1024]{1,0:T(8,128)S(1)} %copy-done.182, f32[1024]{0:T(1024)S(1)} %copy-done.163), kind=kOutput, calls=%fused_computation.21 | convolution fusion | flops 5404094464 | bytes 26775552 | tf_op jit(solution)/shard_map/rd,xdc->rxc/dot_general | solution.py:1107
  433.7 11.7 %fusion.41 = (f32[1024]{0:T(1024)S(1)}, f32[640]{0:T(1024)S(1)}, f32[640]{0:T(1024)S(1)}, f32[1024]{0:T(1024)S(1)}, f32[640,1024,1]{1,0,2:T(8,128)}) fusion(f32[640,1024]{1,0:T(8,128)} %copy-done.19, f32[640]{0:T(1024)S(1)} %add_rsqrt_fusion, f32[640]{0:T(1024)S(1)} %broadcast_multiply_fusion.8, f32[1024]{0:T(1024)S(1)} %copy-done.165, ...), kind=kOutput, calls=%fused_computation.85 | convolution fusion | flops 5374604288 | bytes 18896896 | tf_op jit(solution)/shard_map/rxi,xoi->ro/dot_general | solution.py:1110
  445.5 13.5 %multiply_reduce_fusion.7 = (f32[1024]{0:T(1024)S(1)}, f32[1024]{0:T(1024)S(1)}, f32[1024]{0:T(1024)S(1)}, f32[1024]{0:T(1024)S(1)}, f32[640,1024]{1,0:T(8,128)}, /*index=5*/f32[640,1024,1]{1,0,2:T(8,128)}) fusion(f32[640,1024]{1,0:T(8,128)} %fusion.104, f32[1024]{0:T(1024)S(1)} %copy-done.173, f32[1024]{0:T(1024)S(1)} %copy-done.163, ...), kind=kOutput, calls=%fused_computation.104 | convolution fusion | flops 5380501504 | bytes 29407232 | tf_op jit(solution)/shard_map/rxi,xoi->ro/dot_general | solution.py:1110
  531.0 5.3 multiply_reduce_fusion.9
  540.7 15.2 %convert_reduce_fusion.1 = (f32[2,2048]{1,0:T(2,128)S(1)}, bf16[640,2,2048]{2,0,1:T(8,128)(2,1)}) fusion(f32[640,2,2048]{2,0,1:T(8,128)} %get-tuple-element.157, f32[2,2048]{1,0:T(2,128)S(1)} %copy-done.155, bf16[2,1024,6144]{2,1,0:T(8,128)(2,1)} %bitcast.444, f32[640,1024]{1,0:T(8,128)S(1)} %get-tuple-element.103, f32[1024]{0:T(1024)S(1)} %copy-done.137), kind=kOutput, calls=%fused_computation.22 | convolution fusion | flops 5404094464 | bytes 26775552 | tf_op jit(solution)/shard_map/rd,xdc->rxc/dot_general | solution.py:1107
  558.6 11.4 %fusion.40 = (f32[1024]{0:T(1024)S(1)}, f32[640]{0:T(1024)S(1)}, f32[640]{0:T(1024)S(1)}, f32[1024]{0:T(1024)S(1)}, f32[640,1024,1]{1,0,2:T(8,128)}) fusion(f32[640,1024]{1,0:T(8,128)S(1)} %copy-done.6, f32[640]{0:T(1024)S(1)} %copy-done.150, f32[640]{0:T(1024)S(1)} %copy-done.110, f32[1024]{0:T(1024)S(1)} %copy-done.140, ...), kind=kOutput, calls=%fused_computation.79 | convolution fusion | flops 5374604288 | bytes 18896896 | tf_op jit(solution)/shard_map/rxi,xoi->ro/dot_general | solution.py:1110
  570.7 5.4 multiply_reduce_fusion.11
  608.0 5.3 fusion.72
  632.1 5.0 bitcast_dynamic-update-slice_fusion.11
  647.5 9.7 bitcast_dynamic-update-slice_fusion.3
  657.2 9.3 bitcast_dynamic-update-slice_fusion.2
  666.5 33.1 %copy.355 = bf16[2,1024,6144]{2,1,0:T(8,128)(2,1)} copy(bf16[2,1024,6144]{1,2,0:T(8,128)(2,1)} %bitcast_dynamic-update-slice_fusion.2) | data formatting | bytes 50331648 | tf_op jit(solution)/shard_map/concatenate | solution.py:1191
  712.8 9.7 bitcast_dynamic-update-slice_fusion.1
  722.5 9.5 bitcast_dynamic-update-slice_fusion
  732.0 32.7 %copy.362 = bf16[2,1024,6144]{2,1,0:T(8,128)(2,1)} copy(bf16[2,1024,6144]{1,2,0:T(8,128)(2,1)} %bitcast_dynamic-update-slice_fusion) | data formatting | bytes 50331648 | tf_op jit(solution)/shard_map/concatenate | solution.py:1191
  764.7 33.8 %pad_maximum_fusion.grads = bf16[2,2,4,2,2,64,6144]{6,5,4,3,2,1,0:T(8,128)(2,1)} fusion(bf16[1,2,4,2,2,64,6144]{6,5,4,3,2,1,0:T(8,128)(2,1)} %bitcast.437, bf16[1,2,4,2,2,64,6144]{6,5,4,3,2,1,0:T(8,128)(2,1)} %bitcast.436), kind=kLoop, calls=%fused_computation.6 | loop fusion | flops 25165824 | bytes 100663296 | tf_op jit(solution)/shard_map/stack | solution.py:1194
  798.5 264.7 %scatter_all.1 = (f32[2,64,6144]{2,1,0:T(8,128)}, f32[16,128]{1,0:T(8,128)}, bf16[2,320,1024]{2,1,0:T(8,128)(2,1)}, bf16[2,320,1024]{2,1,0:T(8,128)(2,1)}) custom-call(bf16[2,2,4,2,2,64,6144]{6,5,4,3,2,1,0:T(8,128)(2,1)} %pad_maximum_fusion.grads, f32[2,2,2,4,16,128]{5,4,3,2,1,0:T(8,128)} %bitcast.512, bf16[2,320,1024]{2,1,0:T(8,128)(2,1)} %bitcast.510, ...), custom_call_target="tpu_custom_call" | custom-call | tf_op jit(solution)/shard_map/scatter_all/pallas_call | solution.py:1016
  (650 shorter events, 289.4 us)
Async XLA Ops:
  233.0 98.1 %copy-start.139 = (f32[1024]{0:T(1024)}, f32[1024]{0:T(1024)S(1)}, u32[]{:S(2)}) copy-start(f32[1024]{0:T(1024)S(1)} %mul.503) | copy-start | bytes 12292
  233.1 110.0 %copy-start.136 = (f32[1024]{0:T(1024)}, f32[1024]{0:T(1024)S(1)}, u32[]{:S(2)}) copy-start(f32[1024]{0:T(1024)S(1)} %mul.498) | copy-start | bytes 12292
  242.3 88.8 %copy-start.154 = (f32[2,2048]{1,0:T(2,128)}, f32[2,2048]{1,0:T(2,128)S(1)}, u32[]{:S(2)}) copy-start(f32[2,2048]{1,0:T(2,128)S(1)} %add.313) | copy-start | bytes 49156
  245.8 49.6 %copy-start.43 = (bf16[640,1024,1]{1,0,2:T(8,128)(2,1)}, bf16[640,1024,1]{1,0,2:T(8,128)(2,1)S(1)}, u32[]{:S(2)}) copy-start(bf16[640,1024,1]{1,0,2:T(8,128)(2,1)S(1)} %fusion.130) | copy-start | bytes 3932164
  330.6 12.5 %copy-start.5 = (f32[640,1024]{1,0:T(8,128)}, f32[640,1024]{1,0:T(8,128)S(1)}, u32[]{:S(2)}) copy-start(f32[640,1024]{1,0:T(8,128)S(1)} %get-tuple-element.111) | copy-start | bytes 7864324
  368.5 26.5 %copy-start.33 = (bf16[224,1024]{0,1:T(8,128)(2,1)}, bf16[224,1024]{0,1:T(8,128)(2,1)S(1)}, u32[]{:S(2)}) copy-start(bf16[224,1024]{0,1:T(8,128)(2,1)S(1)} %slice.489) | copy-start | bytes 1376260
  408.6 36.9 %copy-start.152 = (f32[640]{0:T(1024)}, f32[640]{0:T(1024)S(1)}, u32[]{:S(2)}) copy-start(f32[640]{0:T(1024)S(1)} %broadcast_multiply_fusion.8) | copy-start | bytes 7684
  409.3 36.2 %copy-start.178 = (f32[640]{0:T(1024)}, f32[640]{0:T(1024)S(1)}, u32[]{:S(2)}) copy-start(f32[640]{0:T(1024)S(1)} %add_rsqrt_fusion) | copy-start | bytes 7684
  445.5 15.7 %copy-start.176 = (s32[640]{0:T(1024)S(1)}, s32[640]{0:T(1024)}, u32[]{:S(2)}) copy-start(s32[640]{0:T(1024)} %select_add_fusion) | copy-start | bytes 7684
  540.6 15.3 %copy-start.7 = (f32[640,1024]{1,0:T(8,128)}, f32[640,1024]{1,0:T(8,128)S(1)}, u32[]{:S(2)}) copy-start(f32[640,1024]{1,0:T(8,128)S(1)} %get-tuple-element.103) | copy-start | bytes 7864324
  540.6 16.1 %copy-start.115 = (f32[1,1,16,64]{3,1,0,2:T(1,128)S(1)}, f32[1,1,16,64]{3,1,0,2:T(1,128)}, u32[]{:S(2)}) copy-start(f32[1,1,16,64]{3,1,0,2:T(1,128)} %stack.126) | copy-start | bytes 12292
  540.6 16.1 %copy-start.116 = (f32[1,1,16,64]{3,1,0,2:T(1,128)S(1)}, f32[1,1,16,64]{3,1,0,2:T(1,128)}, u32[]{:S(2)}) copy-start(f32[1,1,16,64]{3,1,0,2:T(1,128)} %stack.127) | copy-start | bytes 12292
  540.6 16.1 %copy-start.117 = (f32[1,1,16,64]{3,1,0,2:T(1,128)S(1)}, f32[1,1,16,64]{3,1,0,2:T(1,128)}, u32[]{:S(2)}) copy-start(f32[1,1,16,64]{3,1,0,2:T(1,128)} %stack.129) | copy-start | bytes 12292
  540.6 17.7 %copy-start.98 = (f32[1,2,32,16,4]{2,3,4,1,0:T(8,128)S(1)}, f32[1,2,32,16,4]{2,3,4,1,0:T(8,128)}, u32[]{:S(2)}) copy-start(f32[1,2,32,16,4]{2,3,4,1,0:T(8,128)} %copy.372) | copy-start | bytes 49156
  540.6 17.9 %copy-start.6 = (f32[640,1024]{1,0:T(8,128)S(1)}, f32[640,1024]{1,0:T(8,128)}, u32[]{:S(2)}) copy-start(f32[640,1024]{1,0:T(8,128)} %copy-done.5) | copy-start | bytes 7864324
  540.6 17.9 %copy-start.110 = (f32[640]{0:T(1024)S(1)}, f32[640]{0:T(1024)}, u32[]{:S(2)}) copy-start(f32[640]{0:T(1024)} %copy-done.109) | copy-start | bytes 7684
  540.6 17.9 %copy-start.140 = (f32[1024]{0:T(1024)S(1)}, f32[1024]{0:T(1024)}, u32[]{:S(2)}) copy-start(f32[1024]{0:T(1024)} %copy-done.139) | copy-start | bytes 12292
  540.7 17.9 %copy-start.150 = (f32[640]{0:T(1024)S(1)}, f32[640]{0:T(1024)}, u32[]{:S(2)}) copy-start(f32[640]{0:T(1024)} %copy-done.149) | copy-start | bytes 7684
  644.2 13.0 %slice-start.2 = ((s8[5242880]{0:T(1024)(128)(4,1)}), s8[4194304]{0:T(1024)(128)(4,1)S(1)}, s32[]{:S(2)}) async-start(s8[5242880]{0:T(1024)(128)(4,1)} %bitcast.571), calls=%async_computation.2 | async-start | bytes 8388608
  666.5 33.1 %copy-start.47 = (bf16[640,1024,1]{1,0,2:T(8,128)(2,1)S(1)}, bf16[640,1024,1]{1,0,2:T(8,128)(2,1)}, u32[]{:S(2)}) copy-start(bf16[640,1024,1]{1,0,2:T(8,128)(2,1)} %copy-done.45) | copy-start | bytes 3932164
  666.5 33.1 %copy-start.82 = (bf16[224,2,512]{2,0,1:T(8,128)(2,1)S(1)}, bf16[224,2,512]{2,0,1:T(8,128)(2,1)}, u32[]{:S(2)}) copy-start(bf16[224,2,512]{2,0,1:T(8,128)(2,1)} %copy-done.81) | copy-start | bytes 1376260
  666.5 33.1 %copy-start.93 = (bf16[208,2,512]{2,0,1:T(8,128)(2,1)S(1)}, bf16[208,2,512]{2,0,1:T(8,128)(2,1)}, u32[]{:S(2)}) copy-start(bf16[208,2,512]{2,0,1:T(8,128)(2,1)} %copy.324) | copy-start | bytes 1277956
  666.5 33.1 %copy-start.96 = (bf16[208,2,512]{2,0,1:T(8,128)(2,1)S(1)}, bf16[208,2,512]{2,0,1:T(8,128)(2,1)}, u32[]{:S(2)}) copy-start(bf16[208,2,512]{2,0,1:T(8,128)(2,1)} %copy.323) | copy-start | bytes 1277956
  709.5 13.0 %slice-start = ((s8[5242880]{0:T(1024)(128)(4,1)}), s8[4194304]{0:T(1024)(128)(4,1)S(1)}, s32[]{:S(2)}) async-start(s8[5242880]{0:T(1024)(128)(4,1)} %bitcast.569), calls=%async_computation | async-start | bytes 8388608
  (169 other events, 691.1 us)

commit v2 on v1

--- a/solution.py
+++ b/solution.py
@@ -729,11 +729,11 @@
         slot = self.slot(step)
         return (
             pltpu.make_async_remote_copy(
-                src_ref=self.grads.at[layer, :, :, :, 1 - self.place.c, :, cols], dst_ref=self.near.at[slot],
+                src_ref=self.grads.at[layer, :, :, :, 1 - self.place.c, :, cols], dst_ref=self.acc.at[slot],
                 send_sem=self.send.at[step, len(ROUTES), 0], recv_sem=self.recv.at[step, len(ROUTES), 0],
                 device_id=self.place.other("c"), device_id_type=MESH),
             pltpu.make_async_copy(
-                self.grads.at[layer, :, :, :, self.place.c, :, cols], self.acc.at[slot], self.local.at[step]),
+                self.grads.at[layer, :, :, :, self.place.c, :, cols], self.near, self.local.at[step]),
         )
 
     def core_add(self, step):
@@ -741,7 +741,7 @@
 
         def one(n, carry):
             x, z, y = n // 8, lax.rem(n // 2, 4), lax.rem(n, 2)
-            self.acc[slot, x, z, y] = self.acc[slot, x, z, y] + self.near[slot, x, z, y]
+            self.acc[slot, x, z, y] = self.acc[slot, x, z, y] + self.near[x, z, y]
             return carry
 
         lax.fori_loop(0, NX * NZ * NY, one, 0)
@@ -896,7 +896,7 @@
             slot = self.slot(step)
             layer, first = self.spot(step)
             place = self.place
-            self.summed[layer, :, pl.ds(first, CHUNK)] = self.acc[slot, place.x, place.z, place.y].astype(jnp.float32)
+            self.summed[layer, :, pl.ds(first, CHUNK)] = self.acc[slot, place.x, place.z, place.y]
             self.core_copies(step)[0].wait_send()
             for route in every:
                 for phase in range(3):
@@ -914,8 +914,6 @@
             @pl.when((at >= 0) & (at < self.chunks))
             def _():
                 self.phase(at, number)
-            if number >= 2:
-                pass
         for number in (1, 2, 3):
             at = step - number
 
@@ -942,115 +940,589 @@
     return shapes
 
 
-def rs_kernel(chunks, grads, small, output, tokens_grad, summed, small_sum, out_rows, grad_rows, *scratch):
+WINDOWS = ((0, 208), (208, 208), (416, 224))
+PADDED = 640
+HALF_PAD = 320
+PAIRS = 8
+STEP = 32
+
+
+def swap_halves(place, source, target, odd, n):
+    return (
+        pltpu.make_async_remote_copy(
+            src_ref=source.at[1 - place.x], dst_ref=target.at[place.x],
+            send_sem=odd.at[n], recv_sem=odd.at[n + 1],
+            device_id=place.other("x"), device_id_type=MESH),
+        pltpu.make_async_copy(source.at[place.x], target.at[place.x], odd.at[n + 2]),
+    )
+
+
+class Total:
+    def __init__(self, place, value, landing, send, recv, base):
+        self.place, self.value, self.landing = place, value, landing
+        self.send, self.recv, self.base = send, recv, base
+
+    def copies(self, number):
+        place = self.place
+        if number < 3:
+            slots, devices = [number], [place.other("cxy"[number])]
+        else:
+            slots, devices = [3, 4, 5], [place.device(z=place.along(k)) for k in (1, 2, 3)]
+        return [
+            pltpu.make_async_remote_copy(
+                src_ref=self.value, dst_ref=self.landing.at[slot],
+                send_sem=self.send.at[self.base + slot], recv_sem=self.recv.at[self.base + slot],
+                device_id=device, device_id_type=MESH)
+            for slot, device in zip(slots, devices)
+        ]
+
+    def start(self, number):
+        for copy in self.copies(number):
+            copy.start()
+
+    def add(self, number):
+        for copy in self.copies(number):
+            copy.wait()
+        for slot in ([number] if number < 3 else [3, 4, 5]):
+            self.value[...] = self.value[...] + self.landing[slot]
+
+
+def dot_nn(left, right):
+    return jnp.dot(left, right, preferred_element_type=jnp.float32)
+
+
+def dot_nt(left, right):
+    return lax.dot_general(left, right, (((1,), (1,)), ((), ())), preferred_element_type=jnp.float32)
+
+
+def dot_tn(left, right):
+    return lax.dot_general(left, right, (((0,), (0,)), ((), ())), preferred_element_type=jnp.float32)
+
+
+def both_heads(rows):
+    left = lax.broadcasted_iota(jnp.int32, rows.shape, 1) < 64
+    zero = jnp.zeros_like(rows)
+    return jnp.concatenate([jnp.where(left, rows, zero), jnp.where(left, zero, rows)], axis=0)
+
+
+def one_head_each(rows):
+    n = rows.shape[0] // 2
+    left = lax.broadcasted_iota(jnp.int32, (n, rows.shape[1]), 1) < 64
+    return jnp.where(left, rows[:n], rows[n:])
+
+
+def window_probs(query, keys, other, n):
+    raw = dot_nt(both_heads(query), keys) * 0.125
+    apart = jnp.concatenate([other[:n, :n], other[:n, :n]], axis=0) > 0.5
+    raw = jnp.where(apart, -1e9, raw)
+    powers = jnp.exp(raw - jnp.max(raw, axis=1, keepdims=True))
+    return powers * (1.0 / jnp.sum(powers, axis=1, keepdims=True))
+
+
+def row_loop(body, size=STEP):
+    @pl.loop(0, PADDED // size)
+    def _(n):
+        body(pl.ds(pl.multiple_of(n * size, size), size))
+
+
+def normed_rows(values):
+    centred = values - jnp.mean(values, axis=1, keepdims=True)
+    inverse = lax.rsqrt(jnp.mean(centred * centred, axis=1, keepdims=True) + 1e-06)
+    return centred * inverse, inverse
+
+
+class Weights:
+    def __init__(self, whole, held, sem):
+        self.whole, self.held, self.sem = whole, held, sem
+
+    def copy(self, layer, chunk, x):
+        return pltpu.make_async_copy(
+            self.whole.at[layer, x, :, :, :, :, pl.ds(chunk * CHUNK, CHUNK)], self.held.at[x], self.sem.at[x])
+
+    def start(self, layer, chunk):
+        for x in range(NX):
+            self.copy(layer, chunk, x).start()
+
+    def wait(self, layer, chunk, x):
+        self.copy(layer, chunk, x).wait()
+
+    def get(self, x, first=0, count=CHUNK):
+        return self.held[x, :, :, :, :, first:first + count].reshape(NZ * NY * NC * SHARD, count)
+
+
+def fwd_kernel(
+    layers, shard, small, tokens, cotangent, to_place, other,
+    whole, vec_out, grad_out, resid_out, middle_out, result_out, acts_out, hidden_out, slope_out,
+    mine, mine_grad, vec, small_land, resid, normed, acts, hidden, slope, total, held,
+    send, recv, sib, local, odd, small_send, small_recv, wsem, save,
+):
+    chunks = layers * PER_LAYER
+    place = Place()
+    greet(place)
+    gather = Gather(place, chunks, shard, whole, send, recv, sib, local)
+    weights = Weights(whole, held, wsem)
+    token_copies = swap_halves(place, tokens, mine, odd, 0)
+    grad_copies = swap_halves(place, cotangent, mine_grad, odd, 3)
+    small_total = Total(place, vec, small_land, small_send, small_recv, 0)
+
+    vec[...] = small[...].astype(jnp.float32)
+    small_total.start(0)
+    for copy in token_copies:
+        copy.start()
+    gather.tick(0)
+    small_total.add(0)
+    small_total.start(1)
+    gather.tick(1)
+    for number in (1, 2):
+        small_total.add(number)
+        small_total.start(number + 1)
+    small_total.add(3)
+    for copy in token_copies:
+        copy.wait()
+    for copy in grad_copies:
+        copy.start()
+    vec_copy = pltpu.make_async_copy(vec, vec_out, save.at[12])
+    vec_copy.start()
+    resid[...] = dot_nn(to_place[...], mine[...].reshape(PADDED, -1))
+
+    def early(step, carry):
+        gather.tick(step)
+        return carry
+
+    lax.fori_loop(2, 4 * LAG, early, 0)
+    for copy in grad_copies:
+        copy.wait()
+    slope[0] = dot_nn(to_place[...], mine_grad[...].reshape(PADDED, -1)).astype(jnp.bfloat16)
+    grad_copy = pltpu.make_async_copy(slope.at[0], grad_out, save.at[13])
+    grad_copy.start()
+    grad_copy.wait()
+
+    def one_layer(layer, carry):
+        base = layer * 16
+        row = lambda n: vec[pl.ds(base + n, 1), :]
+
+        def norm_into(gain, shift):
+            def body(rows):
+                values, _ = normed_rows(resid[rows, :])
+                normed[rows, :] = (values * row(gain) + row(shift)).astype(jnp.bfloat16)
+            row_loop(body)
+
+        norm_into(0, 1)
+        resid_copy = pltpu.make_async_copy(resid, resid_out.at[layer], save.at[0])
+        resid_copy.start()
+        gather.tick(layer * PER_LAYER + 4 * LAG)
+        weights.start(layer, 0)
+        for x in range(NX):
+            half = slice(x * 512, x * 512 + 512)
+            weights.wait(layer, 0, x)
+            both = dot_nn(normed[...], weights.get(x))
+            acts[0, :, half] = (both[:, :512] + row(8)[:, half]).astype(jnp.bfloat16)
+            acts[1, :, half] = both[:, 512:].astype(jnp.bfloat16)
+        gather.tick(layer * PER_LAYER + 4 * LAG + 1)
+        weights.start(layer, 1)
+        for x in range(NX):
+            half = slice(x * 512, x * 512 + 512)
+            weights.wait(layer, 1, x)
+            acts[2, :, half] = (dot_nn(normed[...], weights.get(x, 0, 512)) + row(9)[:, half]).astype(jnp.bfloat16)
+
+        @pl.loop(0, PAIRS)
+        def _(pair):
+            lanes = pl.ds(pl.multiple_of(pair * 128, 128), 128)
+            for w, (first, n) in enumerate(WINDOWS):
+                rows = pl.ds(first, n)
+                probs = window_probs(acts[0, rows, lanes], acts[1, rows, lanes], other[w], n)
+                sums = dot_nn(probs.astype(jnp.bfloat16), acts[2, rows, lanes])
+                acts[3, rows, lanes] = one_head_each(sums).astype(jnp.bfloat16)
+
+        acts_copy = pltpu.make_async_copy(acts, acts_out.at[layer], save.at[1])
+        acts_copy.start()
+        total[...] = dot_nt(acts[3, :, :512], weights.get(0, 512, 512)) + dot_nt(acts[3, :, 512:], weights.get(1, 512, 512))
+        resid_copy.wait()
+
+        def to_middle(rows):
+            resid[rows, :] = resid[rows, :] + row(3) * (total[rows, :] + row(2))
+        row_loop(to_middle)
+        middle_copy = pltpu.make_async_copy(resid, middle_out.at[layer], save.at[2])
+        middle_copy.start()
+        norm_into(4, 5)
+        for part in range(2):
+            gather.tick(layer * PER_LAYER + 4 * LAG + 2 + part)
+            weights.start(layer, 2 + part)
+            for x in range(NX):
+                unit = x * 2 + part
+                weights.wait(layer, 2 + part, x)
+                total[...] = dot_nn(normed[...], weights.get(x)) + row(10 + unit)
+                slope_copy = pltpu.make_async_copy(slope.at[x], slope_out.at[layer, unit], save.at[4 + x])
+                if part:
+                    pltpu.make_async_copy(slope.at[x], slope_out.at[layer, unit - 1], save.at[4 + x]).wait()
+
+                def activate(rows):
+                    pre = total[rows, :]
+                    cdf = 0.5 * (1.0 + lax.erf(pre * INV_ROOT_TWO))
+                    pdf = jnp.exp(-0.5 * pre * pre) * INV_ROOT_TAU
+                    hidden[unit, rows, :] = (pre * cdf).astype(jnp.bfloat16)
+                    slope[x, rows, :] = (cdf + pre * pdf).astype(jnp.bfloat16)
+                row_loop(activate, 16)
+                slope_copy.start()
+        hidden_copy = pltpu.make_async_copy(hidden, hidden_out.at[layer], save.at[3])
+        hidden_copy.start()
+        for part in range(2):
+            gather.tick(layer * PER_LAYER + 4 * LAG + 4 + part)
+            weights.start(layer, 4 + part)
+            for x in range(NX):
+                weights.wait(layer, 4 + part, x)
+                term = dot_nt(hidden[x * 2 + part], weights.get(x))
+                if part == 0 and x == 0:
+                    total[...] = term
+                else:
+                    total[...] = total[...] + term
+        middle_copy.wait()
+
+        def to_result(rows):
+            resid[rows, :] = resid[rows, :] + row(7) * (total[rows, :] + row(6))
+        row_loop(to_result)
+        acts_copy.wait()
+        hidden_copy.wait()
+        for x in range(NX):
+            pltpu.make_async_copy(slope.at[x], slope_out.at[layer, x * 2 + 1], save.at[4 + x]).wait()
+        return carry
+
+    lax.fori_loop(0, layers, one_layer, 0)
+    result_copy = pltpu.make_async_copy(resid, result_out, save.at[0])
+    result_copy.start()
+    result_copy.wait()
+    vec_copy.wait()
+
+
+def forward_all(shard, small, tokens, cotangent, to_place, other):
+    layers = shard.shape[0]
+    width = tokens.shape[2]
+    chunks = layers * PER_LAYER
+    any_spec = pl.BlockSpec(memory_space=pl.ANY)
+    full = (PADDED, width)
+    bf16, f32 = jnp.bfloat16, jnp.float32
+    return pl.pallas_call(
+        functools.partial(fwd_kernel, layers),
+        out_shape=(
+            jax.ShapeDtypeStruct((layers, NX, NZ, NY, NC, SHARD, COLS), bf16),
+            jax.ShapeDtypeStruct(small.shape, f32),
+            jax.ShapeDtypeStruct(full, bf16),
+            jax.ShapeDtypeStruct((layers,) + full, f32),
+            jax.ShapeDtypeStruct((layers,) + full, f32),
+            jax.ShapeDtypeStruct(full, f32),
+            jax.ShapeDtypeStruct((layers, 4) + full, bf16),
+            jax.ShapeDtypeStruct((layers, 4) + full, bf16),
+            jax.ShapeDtypeStruct((layers, 4) + full, bf16),
+        ),
+        in_specs=[pl.BlockSpec(memory_space=pltpu.VMEM)] * 6,
+        out_specs=(any_spec,) * 9,
+        scratch_shapes=[
+            pltpu.VMEM(tokens.shape, bf16),
+            pltpu.VMEM(tokens.shape, bf16),
+            pltpu.VMEM(small.shape, f32),
+            pltpu.VMEM((6,) + small.shape, f32),
+            pltpu.VMEM(full, f32),
+            pltpu.VMEM(full, bf16),
+            pltpu.VMEM((4,) + full, bf16),
+            pltpu.VMEM((4,) + full, bf16),
+            pltpu.VMEM((2,) + full, bf16),
+            pltpu.VMEM(full, f32),
+            pltpu.VMEM((NX, NZ, NY, NC, SHARD, CHUNK), bf16),
+            pltpu.SemaphoreType.DMA((chunks, len(ROUTES), 6)),
+            pltpu.SemaphoreType.DMA((chunks, len(ROUTES), 6)),
+            pltpu.SemaphoreType.DMA((2, chunks)),
+            pltpu.SemaphoreType.DMA((chunks,)),
+            pltpu.SemaphoreType.DMA((6,)),
+            pltpu.SemaphoreType.DMA((6,)),
+            pltpu.SemaphoreType.DMA((6,)),
+            pltpu.SemaphoreType.DMA((2,)),
+            pltpu.SemaphoreType.DMA((14,)),
+        ],
+        compiler_params=pltpu.CompilerParams(
+            collective_id=1, has_side_effects=True, vmem_limit_bytes=60 * 1024 * 1024),
+        name="forward_all",
+    )(shard, small, tokens, cotangent, to_place, other)
+
+
+def bwd_kernel(
+    layers, whole, vec, grad_in, resid_in, middle_in, result, acts_in, hidden_in, slope_in, to_place, other,
+    summed, small_sum, out_rows, grad_rows, grads, *scratch,
+):
+    n = len(ROUTES)
     acc, near = scratch[:2]
-    n = len(ROUTES)
     lands = scratch[2:2 + 3 * n]
-    small_acc, small_c, small_x, small_y, small_z, send, recv, local, free, odd = scratch[2 + 3 * n:]
+    (upstream, dy, normed, mid, total, pool, big, held, staged, rows_out, gsum, small_land,
+     send, recv, local, free, odd, small_send, small_recv, wsem, load, stage) = scratch[2 + 3 * n:]
+    chunks = layers * PER_LAYER
     place = Place()
     greet(place)
     scatter = Scatter(place, chunks, grads, summed, acc, near, lands[:n], lands[n:2 * n], lands[2 * n:], send, recv, local, free)
-
-    def halves(n, source, target):
-        return (
-            pltpu.make_async_remote_copy(
-                src_ref=source.at[1 - place.x], dst_ref=target.at[place.x],
-                send_sem=odd.at[4 * n], recv_sem=odd.at[4 * n + 1],
-                device_id=place.other("x"), device_id_type=MESH),
-            pltpu.make_async_copy(source.at[place.x], target.at[place.x], odd.at[4 * n + 2]),
-        )
-
-    def small_copy(source, target, device, base, there=0):
-        return pltpu.make_async_remote_copy(
-            src_ref=source, dst_ref=target, send_sem=odd.at[8 + base], recv_sem=odd.at[16 + there],
-            device_id=device, device_id_type=MESH)
-
-    core = small_copy(small.at[1 - place.c], small_c, place.other("c"), 0, 0)
-    over_x = small_copy(small_acc.at[1 - place.x], small_x, place.other("x"), 1, 1)
-    over_y = small_copy(small_acc.at[place.x, 1 - place.y], small_y, place.other("y"), 2, 2)
-    over_z = [
-        small_copy(small_acc.at[place.x, place.y, place.along(k)], small_z.at[k - 1], place.device(z=place.along(k)), 2 + k, 2 + k)
-        for k in (1, 2, 3)
-    ]
-    rows_copies = halves(0, output, out_rows) + halves(1, tokens_grad, grad_rows)
-    for copy in rows_copies:
+    weights = Weights(whole, held, wsem)
+    out_copies = swap_halves(place, rows_out, out_rows, odd, 0)
+    grad_copies = swap_halves(place, rows_out, grad_rows, odd, 3)
+    small_total = Total(place, small_sum, small_land, small_send, small_recv, 0)
+
+    def fetch(source, target, slot):
+        return pltpu.make_async_copy(source, target, load.at[slot])
+
+    def add_rows(kind, values):
+        gsum[kind] = gsum[kind] + jnp.sum(values.reshape(-1, 8, values.shape[1]), axis=0)
+
+    small_sum[...] = jnp.zeros_like(small_sum)
+    copies = [fetch(result, total, 0), fetch(grad_in, dy, 1)]
+    for copy in copies:
         copy.start()
-    core.start()
-
-    def tick(step, carry):
-        @pl.when(step == 1)
-        def _():
-            core.wait()
-            small_acc[...] = small[place.c] + small_c[...]
-            over_x.start()
-
-        @pl.when(step == 2)
-        def _():
-            over_x.wait()
-            small_acc[place.x] = small_acc[place.x] + small_x[...]
-            over_y.start()
-
-        @pl.when(step == 3)
-        def _():
-            over_y.wait()
-            small_acc[place.x, place.y] = small_acc[place.x, place.y] + small_y[...]
-            for copy in over_z:
-                copy.start()
-        scatter.tick(step)
+    for copy in copies:
+        copy.wait()
+    upstream[...] = dy[...].astype(jnp.float32)
+    pool[0] = total[...].astype(jnp.bfloat16)
+    rows_out[...] = dot_tn(to_place[...], pool[0]).astype(jnp.bfloat16).reshape(rows_out.shape)
+    for copy in out_copies:
+        copy.start()
+
+    def one_layer(turn, carry):
+        layer = layers - 1 - turn
+        base = layer * 16
+        first_step = turn * PER_LAYER
+        row = lambda n: vec[pl.ds(base + n, 1), :]
+        gsum[...] = jnp.zeros_like(gsum)
+
+        def keep(chunk, x):
+            return pltpu.make_async_copy(
+                staged, grads.at[layer, x, :, :, :, :, pl.ds(chunk * CHUNK, CHUNK)], stage.at[0])
+
+        def store(first, values):
+            staged[:, :, :, :, first:first + values.shape[1]] = values.astype(jnp.bfloat16).reshape(
+                NZ, NY, NC, SHARD, values.shape[1])
+
+        middle_copy = fetch(middle_in.at[layer], mid, 0)
+        middle_copy.start()
+        weights.start(layer, 5)
+        middle_copy.wait()
+
+        def first_rows(rows):
+            up = upstream[rows, :]
+            scaled = row(7) * up
+            dy[rows, :] = scaled.astype(jnp.bfloat16)
+            add_rows(6, scaled)
+            middle = mid[rows, :]
+            add_rows(7, up * (total[rows, :] - middle))
+            hat, _ = normed_rows(middle)
+            normed[rows, :] = (hat * row(4) + row(5)).astype(jnp.bfloat16)
+        row_loop(first_rows)
+
+        for turn_part, part in enumerate((1, 0)):
+            reads = [
+                (fetch(hidden_in.at[layer, x * 2 + part], pool.at[x], x),
+                 fetch(slope_in.at[layer, x * 2 + part], pool.at[2 + x], 2 + x)) for x in range(NX)]
+            for pair in reads:
+                for copy in pair:
+                    copy.start()
+            if part == 0:
+                weights.start(layer, 4)
+            for x in range(NX):
+                unit = x * 2 + part
+                for copy in reads[x]:
+                    copy.wait()
+                weights.wait(layer, 4 + part, x)
+                for side in range(2):
+                    store(side * 512, dot_tn(dy[...], pool[x, :, side * 512:side * 512 + 512]))
+                keep(4 + part, x).start()
+                total[...] = dot_nn(dy[...], weights.get(x))
+
+                def to_pre(rows):
+                    grad = (total[rows, :] * pool[2 + x, rows, :].astype(jnp.float32)).astype(jnp.bfloat16)
+                    big[unit, rows, :] = grad
+                    add_rows(10 + unit, grad.astype(jnp.float32))
+                row_loop(to_pre)
+                keep(4 + part, x).wait()
+            scatter.tick(first_step + turn_part)
+        for turn_part, part in enumerate((1, 0)):
+            weights.start(layer, 2 + part)
+            for x in range(NX):
+                unit = x * 2 + part
+                for side in range(2):
+                    store(side * 512, dot_tn(normed[...], big[unit, :, side * 512:side * 512 + 512]))
+                keep(2 + part, x).start()
+                weights.wait(layer, 2 + part, x)
+                term = dot_nt(big[unit], weights.get(x))
+                if turn_part == 0 and x == 0:
+                    total[...] = term
+                else:
+                    total[...] = total[...] + term
+                keep(2 + part, x).wait()
+            scatter.tick(first_step + 2 + turn_part)
+        acts_copy = fetch(acts_in.at[layer], big, 0)
+        acts_copy.start()
+        weights.start(layer, 1)
+
+        def middle_rows(rows):
+            grad = total[rows, :]
+            hat, inverse = normed_rows(mid[rows, :])
+            add_rows(4, grad * hat)
+            add_rows(5, grad)
+            scaled = grad * row(4)
+            inner = (scaled - jnp.mean(scaled, axis=1, keepdims=True)
+                     - hat * jnp.mean(scaled * hat, axis=1, keepdims=True))
+            here = upstream[rows, :] + inverse * inner
+            upstream[rows, :] = here
+            scaled_mid = row(3) * here
+            add_rows(2, scaled_mid)
+            dy[rows, :] = scaled_mid.astype(jnp.bfloat16)
+        row_loop(middle_rows)
+        resid_copy = fetch(resid_in.at[layer], total, 1)
+        resid_copy.start()
+        for x in range(NX):
+            weights.wait(layer, 1, x)
+            pool[0, :, x * 512:x * 512 + 512] = dot_nn(dy[...], weights.get(x, 512, 512)).astype(jnp.bfloat16)
+        resid_copy.wait()
+
+        def resid_rows(rows):
+            values = total[rows, :]
+            add_rows(3, upstream[rows, :] * (mid[rows, :] - values))
+            hat, _ = normed_rows(values)
+            normed[rows, :] = (hat * row(0) + row(1)).astype(jnp.bfloat16)
+        row_loop(resid_rows)
+        acts_copy.wait()
+
+        @pl.loop(0, PAIRS)
+        def _(pair):
+            lanes = pl.ds(pl.multiple_of(pair * 128, 128), 128)
+            for w, (first, n) in enumerate(WINDOWS):
+                rows = pl.ds(first, n)
+                query, keys, values = big[0, rows, lanes], big[1, rows, lanes], big[2, rows, lanes]
+                probs = window_probs(query, keys, other[w], n)
+                grad = both_heads(pool[0, rows, lanes])
+                pool[3, rows, lanes] = dot_tn(probs.astype(jnp.bfloat16), grad).astype(jnp.bfloat16)
+                grad_probs = dot_nt(grad, values)
+                inner = jnp.sum(probs * grad_probs, axis=1, keepdims=True)
+                grad_scores = (probs * (grad_probs - inner)).astype(jnp.bfloat16)
+                pool[1, rows, lanes] = (one_head_each(dot_nn(grad_scores, keys)) * 0.125).astype(jnp.bfloat16)
+                pool[2, rows, lanes] = (dot_tn(grad_scores, both_heads(query)) * 0.125).astype(jnp.bfloat16)
+
+        for x in range(NX):
+            half = slice(x * 512, x * 512 + 512)
+            store(0, dot_tn(normed[...], pool[3, :, half]))
+            store(512, dot_tn(dy[...], big[3, :, half]))
+            keep(1, x).start()
+            term = dot_nt(pool[3, :, half], weights.get(x, 0, 512))
+            mid[...] = term if x == 0 else mid[...] + term
+            keep(1, x).wait()
+        scatter.tick(first_step + 4)
+        weights.start(layer, 0)
+
+        def sum_rows(rows):
+            add_rows(8, pool[1, rows, :].astype(jnp.float32))
+            add_rows(9, pool[3, rows, :].astype(jnp.float32))
+        row_loop(sum_rows)
+        for x in range(NX):
+            half = slice(x * 512, x * 512 + 512)
+            store(0, dot_tn(normed[...], pool[1, :, half]))
+            store(512, dot_tn(normed[...], pool[2, :, half]))
+            keep(0, x).start()
+            weights.wait(layer, 0, x)
+            mid[...] = mid[...] + dot_nt(pool[1, :, half], weights.get(x, 0, 512))
+            mid[...] = mid[...] + dot_nt(pool[2, :, half], weights.get(x, 512, 512))
+            keep(0, x).wait()
+        scatter.tick(first_step + 5)
+
+        def input_rows(rows):
+            grad = mid[rows, :]
+            hat, inverse = normed_rows(total[rows, :])
+            add_rows(0, grad * hat)
+            add_rows(1, grad)
+            scaled = grad * row(0)
+            inner = (scaled - jnp.mean(scaled, axis=1, keepdims=True)
+                     - hat * jnp.mean(scaled * hat, axis=1, keepdims=True))
+            upstream[rows, :] = upstream[rows, :] + inverse * inner
+        row_loop(input_rows)
+        for kind in range(14):
+            value = jnp.sum(gsum[kind], axis=0, keepdims=True)
+            if kind == 3 or kind == 7:
+                value = value / row(kind)
+            small_sum[pl.ds(base + kind, 1), :] = value
         return carry
 
-    lax.fori_loop(0, scatter.ticks, tick, 0)
-    for copy in over_z:
+    lax.fori_loop(0, layers, one_layer, 0)
+    small_total.start(0)
+    for copy in out_copies:
         copy.wait()
-    small_sum[...] = small_acc[place.x, place.y, place.z] + small_z[0] + small_z[1] + small_z[2]
-    for copy in rows_copies:
+    pool[0] = upstream[...].astype(jnp.bfloat16)
+    rows_out[...] = dot_tn(to_place[...], pool[0]).astype(jnp.bfloat16).reshape(rows_out.shape)
+    for copy in grad_copies:
+        copy.start()
+    for number in range(4):
+        scatter.tick(chunks + number)
+        small_total.add(number)
+        if number < 3:
+            small_total.start(number + 1)
+    scatter.tick(chunks + 4)
+    for copy in grad_copies:
         copy.wait()
 
 
-def scatter_all(grads, small, output, tokens_grad):
-    layers = grads.shape[0]
+def backward_all(whole, vec, grad_in, resids, middles, result, acts, hiddens, slopes, to_place, other):
+    layers = whole.shape[0]
+    full = grad_in.shape
+    width = full[1]
     chunks = layers * PER_LAYER
     any_spec = pl.BlockSpec(memory_space=pl.ANY)
     vmem = pl.BlockSpec(memory_space=pltpu.VMEM)
-    tail = small.shape[4:]
+    bf16, f32 = jnp.bfloat16, jnp.float32
+    rows_shape = (2, HALF_PAD, width)
     return pl.pallas_call(
-        functools.partial(rs_kernel, chunks),
+        functools.partial(bwd_kernel, layers),
         out_shape=(
-            jax.ShapeDtypeStruct((layers, SHARD, COLS), jnp.float32),
-            jax.ShapeDtypeStruct(tail, jnp.float32),
-            jax.ShapeDtypeStruct(output.shape, output.dtype),
-            jax.ShapeDtypeStruct(tokens_grad.shape, tokens_grad.dtype),
+            jax.ShapeDtypeStruct((layers, SHARD, COLS), bf16),
+            jax.ShapeDtypeStruct(vec.shape, f32),
+            jax.ShapeDtypeStruct(rows_shape, bf16),
+            jax.ShapeDtypeStruct(rows_shape, bf16),
+            jax.ShapeDtypeStruct(whole.shape, bf16),
         ),
-        in_specs=[any_spec, vmem, vmem, vmem],
-        out_specs=(vmem, vmem, any_spec, any_spec),
+        in_specs=[any_spec, vmem] + [any_spec] * 7 + [vmem, vmem],
+        out_specs=(vmem, vmem, any_spec, any_spec, any_spec),
         scratch_shapes=[
-            pltpu.VMEM((SLOTS, NX, NZ, NY, SHARD, CHUNK), jnp.bfloat16),
-            pltpu.VMEM((SLOTS, NX, NZ, NY, SHARD, CHUNK), jnp.bfloat16),
+            pltpu.VMEM((SLOTS, NX, NZ, NY, SHARD, CHUNK), bf16),
+            pltpu.VMEM((NX, NZ, NY, SHARD, CHUNK), bf16),
         ] + landing_shapes() + [
-            pltpu.VMEM((NX, NY, NZ) + tail, jnp.float32),
-            pltpu.VMEM((NX, NY, NZ) + tail, jnp.float32),
-            pltpu.VMEM((NY, NZ) + tail, jnp.float32),
-            pltpu.VMEM((NZ,) + tail, jnp.float32),
-            pltpu.VMEM((3,) + tail, jnp.float32),
+            pltpu.VMEM(full, f32),
+            pltpu.VMEM(full, bf16),
+            pltpu.VMEM(full, bf16),
+            pltpu.VMEM(full, f32),
+            pltpu.VMEM(full, f32),
+            pltpu.VMEM((4,) + full, bf16),
+            pltpu.VMEM((4,) + full, bf16),
+            pltpu.VMEM((NX, NZ, NY, NC, SHARD, CHUNK), bf16),
+            pltpu.VMEM((NZ, NY, NC, SHARD, CHUNK), bf16),
+            pltpu.VMEM(rows_shape, bf16),
+            pltpu.VMEM((14, 8, width), f32),
+            pltpu.VMEM((6,) + vec.shape, f32),
             pltpu.SemaphoreType.DMA((chunks, len(ROUTES) + 1, 6)),
             pltpu.SemaphoreType.DMA((chunks, len(ROUTES) + 1, 6)),
             pltpu.SemaphoreType.DMA((chunks,)),
             pltpu.SemaphoreType.REGULAR((7,)),
-            pltpu.SemaphoreType.DMA((32,)),
+            pltpu.SemaphoreType.DMA((6,)),
+            pltpu.SemaphoreType.DMA((6,)),
+            pltpu.SemaphoreType.DMA((6,)),
+            pltpu.SemaphoreType.DMA((2,)),
+            pltpu.SemaphoreType.DMA((4,)),
+            pltpu.SemaphoreType.DMA((1,)),
         ],
-        compiler_params=pltpu.CompilerParams(collective_id=2, has_side_effects=True, vmem_limit_bytes=56 * 1024 * 1024),
-        name="scatter_all",
-    )(grads, small, output, tokens_grad)
-
-
-WINDOWS = ((0, 208), (208, 208), (416, 224))
-PADDED = 640
-HALF_PAD = 320
-
-
-def pack_small(vectors, qv_bias, up_bias):
-    flat = jnp.concatenate([vectors.reshape(-1), qv_bias.reshape(-1), up_bias.reshape(-1)])
-    return jnp.pad(flat, (0, 2048 - flat.shape[0])).reshape(16, 128)
+        compiler_params=pltpu.CompilerParams(
+            collective_id=2, has_side_effects=True, vmem_limit_bytes=63 * 1024 * 1024),
+        name="backward_all",
+    )(whole, vec, grad_in, resids, middles, result, acts, hiddens, slopes, to_place, other)
+
+
+def spread_small(vectors, qv_bias, up_bias):
+    layers = vectors.shape[0]
+    here = (jnp.arange(NZ * NY * NC) == lax.axis_index("dp"))
+    side = (jnp.arange(NX) == lax.axis_index("mp"))
+    vec = jnp.where(here[:, None] & side[0], vectors[:, :, None, :], 0).reshape(layers, 8, -1)
+    qv = jnp.where(side[:, None, None, None] & here[:, None], qv_bias[:, :, None, :, None, :], 0).reshape(layers, 2, -1)
+    up = jnp.where(side[:, None, None, None] & here[:, None], up_bias[:, None, :, None, :], 0).reshape(layers, 4, -1)
+    rows = jnp.concatenate([vec, qv, up, jnp.zeros((layers, 2, vec.shape[2]), vec.dtype)], axis=1)
+    return rows.reshape(layers * 16, -1)
 
 
 def placement(ids):
@@ -1076,14 +1548,6 @@
         [qkv_weight[:, 0], qkv_weight[:, 1], qkv_weight[:, 2], jnp.swapaxes(out_weight, 1, 2),
          up_weight, jnp.swapaxes(down_weight, 1, 2)], axis=2)
     extra = ((0, 0), (0, HALF_PAD - half), (0, 0))
-    whole, small_all, mine, mine_grad = gather_all(
-        shard, pack_small(vectors, qv_bias, up_bias), jnp.pad(tokens, extra), jnp.pad(cotangent, extra))
-    weights = whole.reshape(layers, 2, width, COLS)
-    small_flat = small_all.reshape(2, 16, 2048).astype(jnp.float32)
-    vector_all = small_flat[0, :, :1024].reshape(16, layers, 8, 64).transpose(1, 2, 0, 3).reshape(layers, 8, width)
-    qv_all = small_flat[:, :, 1024:1152].reshape(2, 16, layers, 2, 8, 4).transpose(2, 3, 0, 4, 1, 5).reshape(layers, 2, width)
-    up_all = small_flat[:, :, 1152:1408].reshape(2, 16, layers, 32, 4).transpose(2, 0, 3, 1, 4).reshape(layers, 4096)
-
     ids = lax.dynamic_index_in_dim(segments, place_x, 0, keepdims=False)
     position = placement(ids)
     spread = jnp.concatenate([
@@ -1091,121 +1555,21 @@
         jnp.pad(position[half:], (0, HALF_PAD - half), constant_values=-1)])
     to_place = (jnp.arange(PADDED)[:, None] == spread[None, :]).astype(jnp.bfloat16)
     new_ids = jnp.max(jnp.where(jnp.arange(PADDED)[:, None] == position[None, :], ids[None, :], -1), axis=1)
-
-    def sort(rows):
-        return jnp.dot(to_place, rows, preferred_element_type=jnp.float32)
-
-    def unsort(rows):
-        return jnp.dot(to_place.T, rows, preferred_element_type=jnp.float32).astype(jnp.bfloat16)
-
-    resid = sort(mine.reshape(PADDED, width))
-    upstream = sort(mine_grad.reshape(PADDED, width))
-    masks = [(new_ids[a:a + n][:, None] == new_ids[a:a + n][None, :])[None] for a, n in WINDOWS]
-    scale = 0.125
-
-    def project(rows, weight):
-        return jnp.einsum("rd,xdc->rxc", rows, weight, preferred_element_type=jnp.float32).reshape(rows.shape[0], -1)
-
-    def project_t(rows, weight):
-        return jnp.einsum("rxi,xoi->ro", rows.reshape(rows.shape[0], 2, -1), weight, preferred_element_type=jnp.float32)
-
-    def heads(rows, a, n):
-        return rows[a:a + n].reshape(n, 16, 64)
-
-    def probabilities(query, keys, w):
-        a, n = WINDOWS[w]
-        raw = jnp.einsum("qhd,khd->hqk", heads(query, a, n), heads(keys, a, n), preferred_element_type=jnp.float32) * scale
-        raw = jnp.where(masks[w], raw, -1e9)
-        powers = jnp.exp(raw - jnp.max(raw, axis=-1, keepdims=True))
-        return powers / jnp.sum(powers, axis=-1, keepdims=True)
-
-    saves = []
-    for layer in range(layers):
-        w = weights[layer]
-        vec = vector_all[layer]
-        normed_in, n1, r1 = layer_norm(resid, vec[0], vec[1])
-        first = normed_in.astype(jnp.bfloat16)
-        query = (project(first, w[:, :, 0:512]) + qv_all[layer, 0]).astype(jnp.bfloat16)
-        keys = project(first, w[:, :, 512:1024]).astype(jnp.bfloat16)
-        values = (project(first, w[:, :, 1024:1536]) + qv_all[layer, 1]).astype(jnp.bfloat16)
-        parts = []
-        for i, (a, n) in enumerate(WINDOWS):
-            probs = probabilities(query, keys, i).astype(jnp.bfloat16)
-            parts.append(jnp.einsum("hqk,khd->qhd", probs, heads(values, a, n), preferred_element_type=jnp.float32).reshape(n, -1))
-        attended = jnp.concatenate(parts).astype(jnp.bfloat16)
-        projected = project_t(attended, w[:, :, 1536:2048])
-        middle = resid + vec[3] * (projected + vec[2])
-        normed_mid, n2, r2 = layer_norm(middle, vec[4], vec[5])
-        second = normed_mid.astype(jnp.bfloat16)
-        pre = project(second, w[:, :, 2048:4096]) + up_all[layer]
-        hidden = (0.5 * pre * (1.0 + lax.erf(pre * INV_ROOT_TWO))).astype(jnp.bfloat16)
-        returned = project_t(hidden, w[:, :, 4096:])
-        resid = middle + vec[7] * (returned + vec[6])
-        saves.append((n1, r1, first, query, keys, values, attended, projected, n2, r2, second, pre, hidden, returned))
-    output = resid.astype(jnp.bfloat16)
-
-    def grad_w(left, right):
-        n = right.shape[1] // 2
-        return jnp.einsum("rd,rxc->xdc", left, right.reshape(-1, 2, n), preferred_element_type=jnp.float32).astype(jnp.bfloat16)
-
-    all_grads = [None] * layers
-    small_grads = [None] * layers
-    for layer in reversed(range(layers)):
-        w = weights[layer]
-        vec = vector_all[layer]
-        n1, r1, first, query, keys, values, attended, projected, n2, r2, second, pre, hidden, returned = saves[layer]
-        scaled_up = vec[7] * upstream
-        g6 = jnp.sum(scaled_up, axis=0)
-        g7 = jnp.sum(upstream * (returned + vec[6]), axis=0)
-        d_returned = scaled_up.astype(jnp.bfloat16)
-        grad_down = grad_w(d_returned, hidden)
-        d_hidden = project(d_returned, w[:, :, 4096:])
-        cdf = 0.5 * (1.0 + lax.erf(pre * INV_ROOT_TWO))
-        pdf = jnp.exp(-0.5 * pre * pre) * INV_ROOT_TAU
-        d_pre = (d_hidden * (cdf + pre * pdf)).astype(jnp.bfloat16)
-        g_up_bias = jnp.sum(d_pre.astype(jnp.float32), axis=0)
-        grad_up = grad_w(second, d_pre)
-        d_second = project_t(d_pre, w[:, :, 2048:4096])
-        d_mid, g4, g5 = norm_backward(d_second, n2, r2, vec[4])
-        d_middle = upstream + d_mid
-        scaled_mid = vec[3] * d_middle
-        g2 = jnp.sum(scaled_mid, axis=0)
-        g3 = jnp.sum(d_middle * (projected + vec[2]), axis=0)
-        d_projected = scaled_mid.astype(jnp.bfloat16)
-        grad_out = grad_w(d_projected, attended)
-        d_attended = project(d_projected, w[:, :, 1536:2048]).astype(jnp.bfloat16)
-        dq, dk, dv = [], [], []
-        for i, (a, n) in enumerate(WINDOWS):
-            p = probabilities(query, keys, i)
-            da = heads(d_attended, a, n)
-            dv.append(jnp.einsum("hqk,qhd->khd", p.astype(jnp.bfloat16), da, preferred_element_type=jnp.float32).reshape(n, -1))
-            dp = jnp.einsum("qhd,khd->hqk", da, heads(values, a, n), preferred_element_type=jnp.float32)
-            ds = (p * (dp - jnp.sum(p * dp, axis=-1, keepdims=True))).astype(jnp.bfloat16)
-            dq.append((jnp.einsum("hqk,khd->qhd", ds, heads(keys, a, n), preferred_element_type=jnp.float32) * scale).reshape(n, -1))
-            dk.append((jnp.einsum("hqk,qhd->khd", ds, heads(query, a, n), preferred_element_type=jnp.float32) * scale).reshape(n, -1))
-        dq, dk, dv = [jnp.concatenate(v).astype(jnp.bfloat16) for v in (dq, dk, dv)]
-        g_qv = jnp.stack([jnp.sum(dq.astype(jnp.float32), axis=0), jnp.sum(dv.astype(jnp.float32), axis=0)])
-        d_first = project_t(dq, w[:, :, 0:512]) + project_t(dk, w[:, :, 512:1024]) + project_t(dv, w[:, :, 1024:1536])
-        d_in, g0, g1 = norm_backward(d_first, n1, r1, vec[0])
-        upstream = d_middle + d_in
-        all_grads[layer] = jnp.concatenate(
-            [grad_w(first, dq), grad_w(first, dk), grad_w(first, dv), grad_out, grad_up, grad_down], axis=2)
-        small_grads[layer] = (jnp.stack([g0, g1, g2, g3, g4, g5, g6, g7]), g_qv, g_up_bias)
-    grads = jnp.stack(all_grads).reshape(layers, NX, NZ, NY, NC, SHARD, COLS)
-    return finish_fast(grads, small_grads, unsort(output), unsort(upstream.astype(jnp.bfloat16)), half)
-
-
-def finish_fast(grads, small_grads, output, tokens_grad, half):
-    layers = grads.shape[0]
-    width = output.shape[1]
-    vec = jnp.stack([s[0] for s in small_grads]).reshape(layers, 8, 16, 64).transpose(2, 0, 1, 3).reshape(1, 16, 1024)
-    qv = jnp.stack([s[1] for s in small_grads]).reshape(layers, 2, 2, 8, 16, 4).transpose(2, 4, 0, 1, 3, 5).reshape(2, 16, 128)
-    ups = jnp.stack([s[2] for s in small_grads]).reshape(layers, 2, 32, 16, 4).transpose(1, 3, 0, 2, 4).reshape(2, 16, 256)
-    small = jnp.concatenate([jnp.broadcast_to(vec, (2, 16, 1024)), qv, ups, jnp.zeros((2, 16, 640), jnp.float32)], axis=2)
-    small = small.reshape(NX, NZ, NY, NC, 16, 128).transpose(3, 0, 2, 1, 4, 5)
-    summed, small_sum, out_rows, grad_rows = scatter_all(
-        grads, small, output.reshape(2, HALF_PAD, width), tokens_grad.reshape(2, HALF_PAD, width))
-    flat = small_sum.reshape(-1)
+    other = jnp.stack([
+        jnp.pad((new_ids[a:a + n][:, None] != new_ids[a:a + n][None, :]).astype(jnp.float32), ((0, 224 - n), (0, 224 - n)))
+        for a, n in WINDOWS])
+    whole, vec_rows, grad_in, resids, middles, result, acts, hiddens, slopes = forward_all(
+        shard, spread_small(vectors, qv_bias, up_bias), jnp.pad(tokens, extra), jnp.pad(cotangent, extra), to_place, other)
+    summed, small, out_rows, grad_rows, _ = backward_all(
+        whole, vec_rows, grad_in, resids, middles, result, acts, hiddens, slopes, to_place, other)
+    summed = summed.astype(jnp.float32)
+    small = small.reshape(layers, 16, width)
+    dp = lax.axis_index("dp")
+    vec = lax.dynamic_index_in_dim(small[:, :8].reshape(layers, 8, -1, 64), dp, 2, keepdims=False)
+    qv = small[:, 8:10].reshape(layers, 2, NX, -1, NZ * NY * NC, 4)
+    qv = lax.dynamic_index_in_dim(lax.dynamic_index_in_dim(qv, dp, 4, keepdims=False), place_x, 2, keepdims=False)
+    up = small[:, 10:14].reshape(layers, NX, -1, NZ * NY * NC, 4)
+    up = lax.dynamic_index_in_dim(lax.dynamic_index_in_dim(up, dp, 3, keepdims=False), place_x, 1, keepdims=False)
     return (
         out_rows[:, :half],
         grad_rows[:, :half].astype(jnp.float32),
@@ -1213,9 +1577,9 @@
         jnp.swapaxes(summed[:, :, 1536:2048], 1, 2),
         summed[:, :, 2048:4096],
         jnp.swapaxes(summed[:, :, 4096:], 1, 2),
-        flat[:1024].reshape(layers, 8, 64),
-        flat[1024:1152].reshape(layers, 2, 8, 4),
-        flat[1152:1408].reshape(layers, 32, 4),
+        vec,
+        qv,
+        up,
     )
 
 

time: 1090 us -> 681 us (0.62)
  matrix products: 327 us -> 0 us
  local copies, waits for them, and re-layouts: 203 us -> 23.2 us
  Pallas kernels: 483 us -> 643 us
  other arithmetic: 60.7 us -> 6.95 us
    dot_general x70 -> x0, matrix products: 304 us -> none  [the longest x12 84.4 us: project_t(): jnp.einsum('rxi,xoi->ro', rows.reshape(rows.shape[0], 2, -1), weight, pre...]
    pallas_call x2, Pallas kernels: 483 us -> 643 us  [the longest x1 368 us: backward_all(): pl.pallas_call(functools.partial(bwd_kernel, layers), out_shape=(jax.Shap...]
    concatenate x18 -> x0, local copies, waits for them, and re-layouts: 90.8 us -> none  [the longest x2 65.8 us: on_device_fast(): jnp.concatenate([grad_w(first, dq), grad_w(first, dk), grad_w(first, dv),...]
    slice x43 -> x7, local copies, waits for them, and re-layouts: 63.5 us -> 1.33 us  [the longest x1 1.07 us: on_device_fast(): summed[:, :, 2048:4096]]
    another operation x2, other arithmetic: 33.9 us -> 0.96 us  [the longest x1 0.91 us: on_device_fast(): jnp.stack([jnp.pad((new_ids[a:a + n][:, None] != new_ids[a:a + n][None, :...]
    sub x6 -> x0, matrix products: 22.9 us -> none  [probabilities(): powers = jnp.exp(raw - jnp.max(raw, axis=-1, keepdims=True))]
    reduce_sum x10 -> x0, other arithmetic: 15.7 us -> none  [the longest x1 5.35 us: on_device_fast(): g3 = jnp.sum(d_middle * (projected + vec[2]), axis=0)]
    another operation x31 -> x2, local copies, waits for them, and re-layouts: 11.6 us -> 0.06 us  [on_device_fast(): jnp.stack([jnp.pad((new_ids[a:a + n][:, None] != new_ids[a:a + n][None, :...]
where the time goes in v2:
time: 681 us; the launch traced here: 674 us
  Pallas kernels  643 us (94%)
  local copies, waits for them, and re-layouts  23.2 us (3%)
  other arithmetic  6.95 us (1%)
    pallas_call x1, Pallas kernels, backward_all(): pl.pallas_call(functools.partial(bwd_kernel, layers), out_shape=(jax.Shap...  368 us
    pallas_call x1, Pallas kernels, forward_all(): pl.pallas_call(functools.partial(fwd_kernel, layers), out_shape=(jax.Shap...  275 us

profile of v2, /device:TPU:0, one launch (start us, length us, event | category | flops | bytes accessed | tf_op | source)
XLA Modules:
  0.0 674.1 jit_solution(6884189684589146760)
XLA Ops:
  0.7 0.7 copy-done
  2.9 0.9 add_convert_fusion.other
  3.9 0.7 slice_select_fusion
  4.6 1.1 fusion.to_place
  6.5 0.8 broadcast_in_dim.136
  8.5 0.7 pad_maximum_fusion.1
  9.3 1.1 copy-done.4
  10.8 1.1 pad.23.tokens
  12.0 0.8 copy-done.5
  13.1 1.2 pad.24.cotangent
  14.3 275.0 %forward_all.1 = (bf16[2,2,4,2,2,64,6144]{6,5,4,3,2,1,0:T(8,128)(2,1)}, f32[32,1024]{1,0:T(8,128)}, bf16[640,1024]{1,0:T(8,128)(2,1)}, f32[2,640,1024]{2,1,0:T(8...) custom-call(bf16[2,64,6144]{2,1,0:T(8,128)(2,1)} %copy-done.3, ...), custom_call_target="tpu_custom_call" | custom-call | tf_op jit(solution)/shard_map/forward_all/pallas_call | solution.py:1204
  289.3 367.7 %backward_all.1 = (bf16[2,64,6144]{2,1,0:T(8,128)(2,1)}, f32[32,1024]{1,0:T(8,128)}, bf16[2,320,1024]{2,1,0:T(8,128)(2,1)}, bf16[2,320,1024]{2,1,0:T(8,128)(2,1)}, bf16[2,2,4,2,2,64,6144]{6,5,4,3,2,1,0:T(8,128)(2,1)}) custom-call(bf16[2,2,4,2,2,64,6144]{6,5,4,3,2,1,0:T(8,128)(2,1)} %get-tuple-element.22.whole, f32[32,1024]{1,0:T(8,128)} %get-tuple-element.23.vec, ...), custom_call_target="tpu_custom_call" | custom-call | tf_op jit(solution)/shard_map/backward_all/pallas_call | solution.py:1473
  657.0 1.7 convert_element_type.45
  658.7 0.8 slice_bitcast_fusion.1
  659.6 0.9 copy.68
  660.5 0.6 copy-done.7
  661.4 3.4 copy.67
  664.9 1.0 slice_bitcast_fusion
  665.9 0.7 copy-done.6
  666.7 2.3 copy.66
  669.0 1.1 reshape.162
  670.2 0.7 copy.65
  670.8 1.1 slice.88
  672.5 0.7 copy.64
  (80 shorter events, 6.1 us)
Async XLA Ops:
  0.6 0.7 copy-start
  0.7 5.7 copy-start.15
  2.9 4.7 copy-start.13
  3.8 4.5 copy-start.14
  4.6 4.5 copy-start.10
  5.9 3.3 copy-start.11
  6.5 2.7 copy-start.8
  7.4 1.9 copy-start.9
  9.1 1.3 copy-start.4
  10.4 1.6 copy-start.3
  10.8 2.0 copy-start.5
  659.5 1.6 copy-start.7
  664.9 1.7 copy-start.6
  666.7 2.4 copy-start.12
  666.7 4.2 copy-start.2
  670.1 3.8 copy-start.1

commit v3 on v2

--- a/solution.py
+++ b/solution.py
@@ -914,6 +914,8 @@
             @pl.when((at >= 0) & (at < self.chunks))
             def _():
                 self.phase(at, number)
+
+    def pass_on(self, step):
         for number in (1, 2, 3):
             at = step - number
 
@@ -944,7 +946,7 @@
 PADDED = 640
 HALF_PAD = 320
 PAIRS = 8
-STEP = 32
+STEP = 160
 
 
 def swap_halves(place, source, target, odd, n):
@@ -1053,7 +1055,7 @@
 def fwd_kernel(
     layers, shard, small, tokens, cotangent, to_place, other,
     whole, vec_out, grad_out, resid_out, middle_out, result_out, acts_out, hidden_out, slope_out,
-    mine, mine_grad, vec, small_land, resid, normed, acts, hidden, slope, total, held,
+    mine, mine_grad, vec, small_sum, small_land, resid, normed, acts, hidden, slope, total, held,
     send, recv, sib, local, odd, small_send, small_recv, wsem, save,
 ):
     chunks = layers * PER_LAYER
@@ -1063,39 +1065,36 @@
     weights = Weights(whole, held, wsem)
     token_copies = swap_halves(place, tokens, mine, odd, 0)
     grad_copies = swap_halves(place, cotangent, mine_grad, odd, 3)
-    small_total = Total(place, vec, small_land, small_send, small_recv, 0)
-
-    vec[...] = small[...].astype(jnp.float32)
+    small_total = Total(place, small_sum, small_land, small_send, small_recv, 0)
+
+    small_sum[...] = small[...]
     small_total.start(0)
+    gather.tick(0)
+    gather.tick(1)
+    small_total.add(0)
+    small_total.start(1)
     for copy in token_copies:
         copy.start()
-    gather.tick(0)
-    small_total.add(0)
-    small_total.start(1)
-    gather.tick(1)
-    for number in (1, 2):
-        small_total.add(number)
-        small_total.start(number + 1)
-    small_total.add(3)
+    gather.tick(2)
+    gather.tick(3)
+    small_total.add(1)
+    small_total.start(2)
+    gather.tick(4)
+    small_total.add(2)
+    small_total.start(3)
+    gather.tick(5)
+    gather.tick(6)
     for copy in token_copies:
         copy.wait()
     for copy in grad_copies:
         copy.start()
+    gather.tick(7)
+    small_total.add(3)
+    vec[...] = small_sum[...].astype(jnp.float32)
     vec_copy = pltpu.make_async_copy(vec, vec_out, save.at[12])
     vec_copy.start()
     resid[...] = dot_nn(to_place[...], mine[...].reshape(PADDED, -1))
-
-    def early(step, carry):
-        gather.tick(step)
-        return carry
-
-    lax.fori_loop(2, 4 * LAG, early, 0)
-    for copy in grad_copies:
-        copy.wait()
-    slope[0] = dot_nn(to_place[...], mine_grad[...].reshape(PADDED, -1)).astype(jnp.bfloat16)
     grad_copy = pltpu.make_async_copy(slope.at[0], grad_out, save.at[13])
-    grad_copy.start()
-    grad_copy.wait()
 
     def one_layer(layer, carry):
         base = layer * 16
@@ -1110,6 +1109,15 @@
         norm_into(0, 1)
         resid_copy = pltpu.make_async_copy(resid, resid_out.at[layer], save.at[0])
         resid_copy.start()
+
+        @pl.when(layer == layers - 1)
+        def _():
+            for copy in grad_copies:
+                copy.wait()
+            slope[0] = dot_nn(to_place[...], mine_grad[...].reshape(PADDED, -1)).astype(jnp.bfloat16)
+            grad_copy.start()
+            grad_copy.wait()
+
         gather.tick(layer * PER_LAYER + 4 * LAG)
         weights.start(layer, 0)
         for x in range(NX):
@@ -1162,7 +1170,7 @@
                     pdf = jnp.exp(-0.5 * pre * pre) * INV_ROOT_TAU
                     hidden[unit, rows, :] = (pre * cdf).astype(jnp.bfloat16)
                     slope[x, rows, :] = (cdf + pre * pdf).astype(jnp.bfloat16)
-                row_loop(activate, 16)
+                row_loop(activate, 64)
                 slope_copy.start()
         hidden_copy = pltpu.make_async_copy(hidden, hidden_out.at[layer], save.at[3])
         hidden_copy.start()
@@ -1220,7 +1228,8 @@
             pltpu.VMEM(tokens.shape, bf16),
             pltpu.VMEM(tokens.shape, bf16),
             pltpu.VMEM(small.shape, f32),
-            pltpu.VMEM((6,) + small.shape, f32),
+            pltpu.VMEM(small.shape, bf16),
+            pltpu.VMEM((6,) + small.shape, bf16),
             pltpu.VMEM(full, f32),
             pltpu.VMEM(full, bf16),
             pltpu.VMEM((4,) + full, bf16),
@@ -1297,6 +1306,14 @@
 
         middle_copy = fetch(middle_in.at[layer], mid, 0)
         middle_copy.start()
+
+        def reads(part, x):
+            return (fetch(hidden_in.at[layer, x * 2 + part], pool.at[x], 4 + x),
+                    fetch(slope_in.at[layer, x * 2 + part], pool.at[2 + x], 2 + x))
+
+        for x in range(NX):
+            for copy in reads(1, x):
+                copy.start()
         weights.start(layer, 5)
         middle_copy.wait()
 
@@ -1312,40 +1329,42 @@
         row_loop(first_rows)
 
         for turn_part, part in enumerate((1, 0)):
-            reads = [
-                (fetch(hidden_in.at[layer, x * 2 + part], pool.at[x], x),
-                 fetch(slope_in.at[layer, x * 2 + part], pool.at[2 + x], 2 + x)) for x in range(NX)]
-            for pair in reads:
-                for copy in pair:
-                    copy.start()
-            if part == 0:
-                weights.start(layer, 4)
             for x in range(NX):
                 unit = x * 2 + part
-                for copy in reads[x]:
-                    copy.wait()
-                weights.wait(layer, 4 + part, x)
+                hidden_copy, slope_copy = reads(part, x)
+                hidden_copy.wait()
                 for side in range(2):
                     store(side * 512, dot_tn(dy[...], pool[x, :, side * 512:side * 512 + 512]))
                 keep(4 + part, x).start()
+                if part == 1:
+                    reads(0, x)[0].start()
+                weights.wait(layer, 4 + part, x)
                 total[...] = dot_nn(dy[...], weights.get(x))
+                weights.copy(layer, 3 + part, x).start()
+                if x == 0:
+                    scatter.pass_on(first_step + turn_part - 1)
+                slope_copy.wait()
 
                 def to_pre(rows):
                     grad = (total[rows, :] * pool[2 + x, rows, :].astype(jnp.float32)).astype(jnp.bfloat16)
                     big[unit, rows, :] = grad
                     add_rows(10 + unit, grad.astype(jnp.float32))
                 row_loop(to_pre)
+                if part == 1:
+                    reads(0, x)[1].start()
                 keep(4 + part, x).wait()
             scatter.tick(first_step + turn_part)
         for turn_part, part in enumerate((1, 0)):
-            weights.start(layer, 2 + part)
             for x in range(NX):
                 unit = x * 2 + part
                 for side in range(2):
                     store(side * 512, dot_tn(normed[...], big[unit, :, side * 512:side * 512 + 512]))
                 keep(2 + part, x).start()
+                if x == 0:
+                    scatter.pass_on(first_step + 1 + turn_part)
                 weights.wait(layer, 2 + part, x)
                 term = dot_nt(big[unit], weights.get(x))
+                weights.copy(layer, 1 + part, x).start()
                 if turn_part == 0 and x == 0:
                     total[...] = term
                 else:
@@ -1354,7 +1373,6 @@
             scatter.tick(first_step + 2 + turn_part)
         acts_copy = fetch(acts_in.at[layer], big, 0)
         acts_copy.start()
-        weights.start(layer, 1)
 
         def middle_rows(rows):
             grad = total[rows, :]
@@ -1383,6 +1401,7 @@
             hat, _ = normed_rows(values)
             normed[rows, :] = (hat * row(0) + row(1)).astype(jnp.bfloat16)
         row_loop(resid_rows)
+        scatter.pass_on(first_step + 3)
         acts_copy.wait()
 
         @pl.loop(0, PAIRS)
@@ -1406,10 +1425,10 @@
             store(512, dot_tn(dy[...], big[3, :, half]))
             keep(1, x).start()
             term = dot_nt(pool[3, :, half], weights.get(x, 0, 512))
+            weights.copy(layer, 0, x).start()
             mid[...] = term if x == 0 else mid[...] + term
             keep(1, x).wait()
         scatter.tick(first_step + 4)
-        weights.start(layer, 0)
 
         def sum_rows(rows):
             add_rows(8, pool[1, rows, :].astype(jnp.float32))
@@ -1420,6 +1439,8 @@
             store(0, dot_tn(normed[...], pool[1, :, half]))
             store(512, dot_tn(normed[...], pool[2, :, half]))
             keep(0, x).start()
+            if x == 0:
+                scatter.pass_on(first_step + 4)
             weights.wait(layer, 0, x)
             mid[...] = mid[...] + dot_nt(pool[1, :, half], weights.get(x, 0, 512))
             mid[...] = mid[...] + dot_nt(pool[2, :, half], weights.get(x, 512, 512))
@@ -1452,10 +1473,12 @@
     for copy in grad_copies:
         copy.start()
     for number in range(4):
+        scatter.pass_on(chunks + number - 1)
         scatter.tick(chunks + number)
         small_total.add(number)
         if number < 3:
             small_total.start(number + 1)
+    scatter.pass_on(chunks + 3)
     scatter.tick(chunks + 4)
     for copy in grad_copies:
         copy.wait()
@@ -1505,7 +1528,7 @@
             pltpu.SemaphoreType.DMA((6,)),
             pltpu.SemaphoreType.DMA((6,)),
             pltpu.SemaphoreType.DMA((2,)),
-            pltpu.SemaphoreType.DMA((4,)),
+            pltpu.SemaphoreType.DMA((6,)),
             pltpu.SemaphoreType.DMA((1,)),
         ],
         compiler_params=pltpu.CompilerParams(

time: 681 us -> 597 us (0.88)
  Pallas kernels: 643 us -> 557 us
    pallas_call x1, Pallas kernels: 368 us -> 313 us  [backward_all(): pl.pallas_call(functools.partial(bwd_kernel, layers), out_shape=(jax.Shap...]
    pallas_call x1, Pallas kernels: 275 us -> 243 us  [forward_all(): pl.pallas_call(functools.partial(fwd_kernel, layers), out_shape=(jax.Shap...]
where the time goes in v3:
time: 597 us; the launch traced here: 588 us
  Pallas kernels  557 us (93%)
  local copies, waits for them, and re-layouts  23.2 us (4%)
  other arithmetic  6.95 us (1%)
    pallas_call x1, Pallas kernels, backward_all(): pl.pallas_call(functools.partial(bwd_kernel, layers), out_shape=(jax.Shap...  313 us
    pallas_call x1, Pallas kernels, forward_all(): pl.pallas_call(functools.partial(fwd_kernel, layers), out_shape=(jax.Shap...  243 us

profile of v3, /device:TPU:0, one launch (start us, length us, event | category | flops | bytes accessed | tf_op | source)
XLA Modules:
  0.0 588.3 jit_solution(6846774565250563476)
XLA Ops:
  0.7 0.7 copy-done
  2.9 0.9 add_convert_fusion.other
  3.9 0.7 slice_select_fusion
  4.6 1.1 fusion.to_place
  6.5 0.8 broadcast_in_dim.136
  8.5 0.7 pad_maximum_fusion.1
  9.3 1.1 copy-done.4
  10.8 1.1 pad.23.tokens
  12.0 0.8 copy-done.5
  13.1 1.2 pad.24.cotangent
  14.3 243.2 %forward_all.1 = (bf16[2,2,4,2,2,64,6144]{6,5,4,3,2,1,0:T(8,128)(2,1)}, f32[32,1024]{1,0:T(8,128)}, bf16[640,1024]{1,0:T(8,128)(2,1)}, f32[2,640,1024]{2,1,0:T(8...) custom-call(bf16[2,64,6144]{2,1,0:T(8,128)(2,1)} %copy-done.3, ...), custom_call_target="tpu_custom_call" | custom-call | tf_op jit(solution)/shard_map/forward_all/pallas_call | solution.py:1212
  257.5 313.4 %backward_all.1 = (bf16[2,64,6144]{2,1,0:T(8,128)(2,1)}, f32[32,1024]{1,0:T(8,128)}, bf16[2,320,1024]{2,1,0:T(8,128)(2,1)}, bf16[2,320,1024]{2,1,0:T(8,128)(2,1)}, bf16[2,2,4,2,2,64,6144]{6,5,4,3,2,1,0:T(8,128)(2,1)}) custom-call(bf16[2,2,4,2,2,64,6144]{6,5,4,3,2,1,0:T(8,128)(2,1)} %get-tuple-element.22.whole, f32[32,1024]{1,0:T(8,128)} %get-tuple-element.23.vec, ...), custom_call_target="tpu_custom_call" | custom-call | tf_op jit(solution)/shard_map/backward_all/pallas_call | solution.py:1496
  570.9 1.7 convert_element_type.45
  572.7 0.8 slice_bitcast_fusion.1
  573.5 0.9 copy.68
  574.4 0.6 copy-done.7
  575.4 3.4 copy.67
  578.8 1.0 slice_bitcast_fusion
  579.8 0.7 copy-done.6
  580.6 2.3 copy.66
  582.9 1.1 reshape.162
  584.1 0.7 copy.65
  584.7 1.1 slice.88
  586.4 0.7 copy.64
  (80 shorter events, 6.1 us)
Async XLA Ops:
  0.6 0.7 copy-start
  0.7 5.7 copy-start.15
  2.9 4.7 copy-start.13
  3.8 4.5 copy-start.14
  4.6 4.5 copy-start.10
  5.9 3.3 copy-start.11
  6.5 2.7 copy-start.8
  7.4 1.9 copy-start.9
  9.1 1.3 copy-start.4
  10.4 1.6 copy-start.3
  10.8 2.0 copy-start.5
  573.4 1.6 copy-start.7
  578.8 1.7 copy-start.6
  580.6 2.4 copy-start.12
  580.6 4.2 copy-start.2
  584.0 3.8 copy-start.1

commit v4 on v3

--- a/solution.py
+++ b/solution.py
@@ -896,7 +896,7 @@
             slot = self.slot(step)
             layer, first = self.spot(step)
             place = self.place
-            self.summed[layer, :, pl.ds(first, CHUNK)] = self.acc[slot, place.x, place.z, place.y]
+            self.store(layer, lax.rem(self.chunks - 1 - step, PER_LAYER), self.acc[slot, place.x, place.z, place.y])
             self.core_copies(step)[0].wait_send()
             for route in every:
                 for phase in range(3):
@@ -906,6 +906,29 @@
             def _():
                 for device, there, _ in self.others():
                     pl.semaphore_signal(self.free.at[there], inc=1, device_id=device, device_id_type=MESH)
+
+    def store(self, layer, chunk, values):
+        qkv, out, up, down = self.summed
+        side = CHUNK // 2
+
+        @pl.when(chunk == 0)
+        def _():
+            qkv[layer, 0] = values[:, :side]
+            qkv[layer, 1] = values[:, side:]
+
+        @pl.when(chunk == 1)
+        def _():
+            qkv[layer, 2] = values[:, :side]
+            out[layer] = values[:, side:].astype(jnp.float32).T.astype(jnp.bfloat16)
+
+        @pl.when((chunk == 2) | (chunk == 3))
+        def _():
+            up[layer, :, pl.ds(pl.multiple_of((chunk - 2) * CHUNK, CHUNK), CHUNK)] = values
+
+        @pl.when(chunk >= 4)
+        def _():
+            down[layer, pl.ds(pl.multiple_of((chunk - 4) * CHUNK, CHUNK), CHUNK), :] = (
+                values.astype(jnp.float32).T.astype(jnp.bfloat16))
 
     def tick(self, step):
         for number in (4, 3, 2, 1, 0):
@@ -1255,7 +1278,7 @@
 
 def bwd_kernel(
     layers, whole, vec, grad_in, resid_in, middle_in, result, acts_in, hidden_in, slope_in, to_place, other,
-    summed, small_sum, out_rows, grad_rows, grads, *scratch,
+    qkv_sum, out_sum, up_sum, down_sum, small_sum, out_rows, grad_rows, grads, *scratch,
 ):
     n = len(ROUTES)
     acc, near = scratch[:2]
@@ -1265,7 +1288,9 @@
     chunks = layers * PER_LAYER
     place = Place()
     greet(place)
-    scatter = Scatter(place, chunks, grads, summed, acc, near, lands[:n], lands[n:2 * n], lands[2 * n:], send, recv, local, free)
+    scatter = Scatter(
+        place, chunks, grads, (qkv_sum, out_sum, up_sum, down_sum), acc, near,
+         lands[:n], lands[n:2 * n], lands[2 * n:], send, recv, local, free)
     weights = Weights(whole, held, wsem)
     out_copies = swap_halves(place, rows_out, out_rows, odd, 0)
     grad_copies = swap_halves(place, rows_out, grad_rows, odd, 3)
@@ -1496,14 +1521,17 @@
     return pl.pallas_call(
         functools.partial(bwd_kernel, layers),
         out_shape=(
-            jax.ShapeDtypeStruct((layers, SHARD, COLS), bf16),
+            jax.ShapeDtypeStruct((layers, 3, SHARD, CHUNK // 2), bf16),
+            jax.ShapeDtypeStruct((layers, CHUNK // 2, SHARD), bf16),
+            jax.ShapeDtypeStruct((layers, SHARD, 2 * CHUNK), bf16),
+            jax.ShapeDtypeStruct((layers, 2 * CHUNK, SHARD), bf16),
             jax.ShapeDtypeStruct(vec.shape, f32),
             jax.ShapeDtypeStruct(rows_shape, bf16),
             jax.ShapeDtypeStruct(rows_shape, bf16),
             jax.ShapeDtypeStruct(whole.shape, bf16),
         ),
         in_specs=[any_spec, vmem] + [any_spec] * 7 + [vmem, vmem],
-        out_specs=(vmem, vmem, any_spec, any_spec, any_spec),
+        out_specs=(vmem,) * 5 + (any_spec,) * 3,
         scratch_shapes=[
             pltpu.VMEM((SLOTS, NX, NZ, NY, SHARD, CHUNK), bf16),
             pltpu.VMEM((NX, NZ, NY, SHARD, CHUNK), bf16),
@@ -1583,9 +1611,8 @@
         for a, n in WINDOWS])
     whole, vec_rows, grad_in, resids, middles, result, acts, hiddens, slopes = forward_all(
         shard, spread_small(vectors, qv_bias, up_bias), jnp.pad(tokens, extra), jnp.pad(cotangent, extra), to_place, other)
-    summed, small, out_rows, grad_rows, _ = backward_all(
+    qkv_sum, out_sum, up_sum, down_sum, small, out_rows, grad_rows, _ = backward_all(
         whole, vec_rows, grad_in, resids, middles, result, acts, hiddens, slopes, to_place, other)
-    summed = summed.astype(jnp.float32)
     small = small.reshape(layers, 16, width)
     dp = lax.axis_index("dp")
     vec = lax.dynamic_index_in_dim(small[:, :8].reshape(layers, 8, -1, 64), dp, 2, keepdims=False)
@@ -1596,10 +1623,10 @@
     return (
         out_rows[:, :half],
         grad_rows[:, :half].astype(jnp.float32),
-        jnp.stack([summed[:, :, 0:512], summed[:, :, 512:1024], summed[:, :, 1024:1536]], axis=1),
-        jnp.swapaxes(summed[:, :, 1536:2048], 1, 2),
-        summed[:, :, 2048:4096],
-        jnp.swapaxes(summed[:, :, 4096:], 1, 2),
+        qkv_sum.astype(jnp.float32),
+        out_sum.astype(jnp.float32),
+        up_sum.astype(jnp.float32),
+        down_sum.astype(jnp.float32),
         vec,
         qv,
         up,

time: 597 us -> 590 us (0.988)
  no operation moved by 1% of the time
where the time goes in v4:
time: 590 us; the launch traced here: 583 us
  Pallas kernels  553 us (94%)
  local copies, waits for them, and re-layouts  20.2 us (3%)
  other arithmetic  8.56 us (1%)
    pallas_call x1, Pallas kernels, backward_all(): pl.pallas_call(functools.partial(bwd_kernel, layers), out_shape=(jax.Shap...  310 us
    pallas_call x1, Pallas kernels, forward_all(): pl.pallas_call(functools.partial(fwd_kernel, layers), out_shape=(jax.Shap...  243 us

profile of v4, /device:TPU:0, one launch (start us, length us, event | category | flops | bytes accessed | tf_op | source)
XLA Modules:
  0.0 583.2 jit_solution(6943048659073713576)
XLA Ops:
  0.7 0.7 copy-done
  2.9 0.9 add_convert_fusion.other
  3.9 0.7 slice_select_fusion
  4.6 1.1 fusion.to_place
  6.5 0.8 broadcast_in_dim.136
  8.5 0.7 pad_maximum_fusion
  9.3 1.1 copy-done.3
  10.8 1.2 pad.23.tokens
  12.0 0.8 copy-done.4
  13.1 1.2 pad.24.cotangent
  14.3 243.2 %forward_all.1 = (bf16[2,2,4,2,2,64,6144]{6,5,4,3,2,1,0:T(8,128)(2,1)}, f32[32,1024]{1,0:T(8,128)}, bf16[640,1024]{1,0:T(8,128)(2,1)}, f32[2,640,1024]{2,1,0:T(8...) custom-call(bf16[2,64,6144]{2,1,0:T(8,128)(2,1)} %copy-done.2, ...), custom_call_target="tpu_custom_call" | custom-call | tf_op jit(solution)/shard_map/forward_all/pallas_call | solution.py:1235
  257.5 309.7 %backward_all.1 = (bf16[2,3,64,512]{3,2,1,0:T(8,128)(2,1)}, bf16[2,512,64]{2,1,0:T(8,128)(2,1)}, bf16[2,64,2048]{2,1,0:T(8,128)(2,1)}, bf16[2,2048,64]{2,1,0:T(8...) custom-call(bf16[2,2,4,2,2,64,6144]{6,5,4,3,2,1,0:T(8,128)(2,1)} %ge, ...), custom_call_target="tpu_custom_call" | custom-call | tf_op jit(solution)/shard_map/backward_all/pallas_call | solution.py:1521
  567.1 1.6 slice_convert_fusion
  568.8 3.4 copy.70
  572.3 2.3 copy.69
  574.7 1.1 reshape.162
  575.8 0.7 copy.68
  576.5 1.1 convert_element_type.56
  577.5 1.3 copy.72
  578.9 1.0 convert_element_type.54
  579.9 0.5 reshape.161
  580.4 0.7 copy.67
  581.1 0.8 copy.71
  582.0 0.6 constant_dynamic-slice_fusion.2
  (82 shorter events, 4.6 us)
Async XLA Ops:
  0.6 0.7 copy-start
  0.7 5.7 copy-start.17
  2.9 4.7 copy-start.15
  3.8 4.5 copy-start.16
  4.6 4.5 copy-start.10
  5.9 3.3 copy-start.13
  6.5 2.7 copy-start.8
  7.4 1.9 copy-start.9
  9.1 1.3 copy-start.3
  10.4 1.6 copy-start.2
  10.8 2.0 copy-start.4
  568.8 3.4 copy-start.5
  572.3 2.4 copy-start.14
  572.3 4.2 copy-start.7
  574.6 2.9 copy-start.6
  576.5 2.4 copy-start.11
  577.5 3.6 copy-start.12
  577.5 5.1 copy-start.1
